TPU v7x, 256 devices: a whole 4x4x8 slice. The times are simulated.
256 devices in a mesh: tile: 64 (over y, z, core), pair: 4 (over x).
Axes of the slice: x: 4, y: 4, z: 8, core: 2. Of those that a mesh axis runs over, the one named last changes fastest.
Arguments:
- fixed_image: bfloat16 [4, 32768, 512], P('pair', 'tile'), may hold values from -6 to 6
- moving_patches: bfloat16 [4, 2048, 160, 160], P('pair', 'tile'), may hold values from -6 to 6
- owners: int32 [4, 2048], P('pair', 'tile'), may hold values from 0 to 63, as said below
- offsets: int32 [4, 2048, 2], P('pair', 'tile'), may hold values from 0 to 352
- mobility: float32 [4, 1024, 512], P('pair', 'tile'), may hold values from 0.3 to 1
- prior_flow: float32 [4, 2, 1024, 512], P('pair', None, 'tile'), may hold values from -4 to 4
Outputs:
- patch_flow: float32 [4, 2, 2048], P('pair', None, 'tile')
- displacement: float32 [4, 2, 1024, 512], P('pair', None, 'tile')
Inputs may be any that keep to these rules, and one draw needn't show every extreme that they name: `owners`: within one section pair, each owner is named by at most 2 patches of any one device's 32 patches and by at most 64 patches in all; both bounds are reached in every draw.
All inputs are finite; a program needn't handle non-finite values.
Results may differ from a plain program's by a relative error of at most 0.015.
Values may be sent and summed in bfloat16 or wider, within the bound.
A program may use at most 128 MiB of HBM per device.

v0:
```python
import math

import jax
import jax.numpy as jnp
from jax import lax
from jax.sharding import PartitionSpec as P

CAP = 2
STEPS = 32


EPS = 1e-06


def extended(value, sides, width):
    for axis, dim in sides:
        peers, length = (lax.axis_size(axis), value.shape[dim])
        up = [(i, (i + 1) % peers) for i in range(peers - 1)]
        down = [(j, i) for i, j in up]
        last = lax.slice_in_dim(value, length - width, length, axis=dim)
        leading = lax.slice_in_dim(value, 0, width, axis=dim)
        before = lax.ppermute(last, axis, up)
        after = lax.ppermute(leading, axis, down)
        value = jnp.concatenate([before, value, after], axis=dim)
    return value


def make_tables(patch_side):
    numbers = jnp.arange(patch_side, dtype=jnp.int32)
    phase = (numbers[:, None] * numbers[None, :] % patch_side).astype(jnp.float32) * (
        2.0 * math.pi / patch_side
    )
    scale = 1.0 / math.sqrt(patch_side)
    return (
        (jnp.cos(phase) * scale).astype(jnp.bfloat16),
        (jnp.sin(phase) * scale).astype(jnp.bfloat16),
    )


def left_mul(table, batch):
    return jnp.einsum("ab,nbc->nac", table, batch, preferred_element_type=jnp.float32)


def right_mul(batch, table):
    return jnp.einsum("nab,bc->nac", batch, table, preferred_element_type=jnp.float32)


def spectrum(batch, cos_table, sin_table):
    a_part = left_mul(cos_table, batch).astype(jnp.bfloat16)
    b_part = left_mul(sin_table, batch).astype(jnp.bfloat16)
    real_part = (right_mul(a_part, cos_table) - right_mul(b_part, sin_table)).astype(jnp.bfloat16)
    imag_part = (-(right_mul(a_part, sin_table) + right_mul(b_part, cos_table))).astype(
        jnp.bfloat16
    )
    return (real_part, imag_part)


def block_flows(fixed_batch, moving_batch, cos_table, sin_table):
    patch_side = fixed_batch.shape[1]
    fixed_re, fixed_im = spectrum(fixed_batch, cos_table, sin_table)
    moving_re, moving_im = spectrum(moving_batch, cos_table, sin_table)
    fr32 = fixed_re.astype(jnp.float32)
    fi32 = fixed_im.astype(jnp.float32)
    mr32 = moving_re.astype(jnp.float32)
    mi32 = moving_im.astype(jnp.float32)
    cross_re = (fr32 * mr32 + fi32 * mi32).astype(jnp.bfloat16)
    cross_im = (fi32 * mr32 - fr32 * mi32).astype(jnp.bfloat16)
    back_re = (left_mul(cos_table, cross_re) - left_mul(sin_table, cross_im)).astype(jnp.bfloat16)
    back_im = (left_mul(cos_table, cross_im) + left_mul(sin_table, cross_re)).astype(jnp.bfloat16)
    correlation = right_mul(back_re, cos_table) - right_mul(back_im, sin_table)
    energy = correlation * correlation
    total_energy = jnp.sum(energy, axis=(1, 2)) + EPS
    numbers = jnp.arange(patch_side, dtype=jnp.int32)
    signed_shift = jnp.where(numbers < patch_side // 2, numbers, numbers - patch_side).astype(
        jnp.float32
    )
    flow_rows = jnp.sum(energy * signed_shift[None, :, None], axis=(1, 2)) / total_energy
    flow_cols = jnp.sum(energy * signed_shift[None, None, :], axis=(1, 2)) / total_energy
    return jnp.stack([flow_rows, flow_cols], axis=1)


def all_flows(fixed_batch, moving_batch, cos_table, sin_table):
    patch_count = fixed_batch.shape[0]
    patch_side = fixed_batch.shape[1]
    block = 8
    grouped_fixed = fixed_batch.reshape(patch_count // block, block, patch_side, patch_side)
    grouped_moving = moving_batch.reshape(patch_count // block, block, patch_side, patch_side)
    results = lax.map(
        lambda pieces: block_flows(pieces[0], pieces[1], cos_table, sin_table),
        (grouped_fixed, grouped_moving),
    )
    return results.reshape(patch_count, 2)


def cut_windows(fixed_tile, first_rows, first_cols, patch_side):

    def cut_one(first_row, first_col):
        return lax.dynamic_slice(fixed_tile, (first_row, first_col), (patch_side, patch_side))

    return jax.vmap(cut_one)(first_rows.astype(jnp.int32), first_cols.astype(jnp.int32))


def shards(fixed_image, moving_patches, owners, offsets, mobility, prior_flow):
    patch_count = moving_patches.shape[1]
    patch_side = moving_patches.shape[2]
    tile_count = lax.axis_size("tile")
    cos_table, sin_table = make_tables(patch_side)
    fixed_tile = fixed_image[0]
    moving = moving_patches[0]
    target_owner = owners[0]
    patch_offsets = offsets[0]
    numbers = jnp.arange(patch_count, dtype=jnp.int32)
    same_owner = target_owner[:, None] == target_owner[None, :]
    earlier = numbers[None, :] < numbers[:, None]
    rank_within = jnp.sum((same_owner & earlier).astype(jnp.int32), axis=1)
    slot_of = target_owner * CAP + rank_within
    slot_count = tile_count * CAP
    slot_numbers = jnp.arange(slot_count, dtype=jnp.int32)
    matches = slot_of[None, :] == slot_numbers[:, None]
    filled = jnp.any(matches, axis=1)
    source_patch = jnp.sum(jnp.where(matches, numbers[None, :], 0), axis=1)
    chosen_offsets = jnp.take(patch_offsets, source_patch, axis=0)
    requests = jnp.stack(
        [
            filled.astype(jnp.int32),
            jnp.where(filled, chosen_offsets[:, 0], 0),
            jnp.where(filled, chosen_offsets[:, 1], 0),
        ],
        axis=1,
    )
    outgoing = jnp.where(
        filled[:, None, None], jnp.take(moving, source_patch, axis=0), jnp.zeros((), jnp.bfloat16)
    )
    arrived, arrived_meta = (
        lax.all_to_all(
            outgoing.reshape(tile_count, CAP, patch_side, patch_side),
            "tile",
            split_axis=0,
            concat_axis=0,
            tiled=True,
        ),
        lax.all_to_all(
            requests.reshape(tile_count, CAP, 3), "tile", split_axis=0, concat_axis=0, tiled=True
        ),
    )
    arrived = arrived.reshape(slot_count, patch_side, patch_side)
    arrived_meta = arrived_meta.reshape(slot_count, 3)
    present = arrived_meta[:, 0]
    placed = (jnp.cumsum(present) - 1).astype(jnp.int32)
    capacity = 2 * patch_count
    compact_numbers = jnp.arange(capacity, dtype=jnp.int32)
    picks = (present[None, :] == 1) & (placed[None, :] == compact_numbers[:, None])
    chosen_slot = jnp.sum(jnp.where(picks, slot_numbers[None, :], 0), axis=1)
    work_moving = jnp.take(arrived, chosen_slot, axis=0)
    work_meta = jnp.take(arrived_meta, chosen_slot, axis=0)
    work_fixed = cut_windows(fixed_tile, work_meta[:, 1], work_meta[:, 2], patch_side)
    results = all_flows(work_fixed, work_moving, cos_table, sin_table)
    returned = jnp.where(
        present[:, None] == 1, jnp.take(results, jnp.clip(placed, 0, capacity - 1), axis=0), 0.0
    )
    homeward = lax.all_to_all(
        returned.reshape(tile_count, CAP, 2), "tile", split_axis=0, concat_axis=0, tiled=True
    )
    flows = jnp.take(homeward.reshape(slot_count, 2), slot_of, axis=0)
    patch_flow = flows.T[None]
    node_rows = prior_flow.shape[2]
    node_cols = prior_flow.shape[3]
    stride_nodes = node_rows * node_cols // patch_count
    extra = (
        jnp.zeros((1, 2, patch_count, stride_nodes), jnp.float32)
        .at[:, :, :, stride_nodes // 2]
        .set(patch_flow)
    )
    target = prior_flow + extra.reshape(1, 2, node_rows, node_cols)
    pair_count = lax.axis_size("pair")
    global_rows = lax.axis_index("tile") * node_rows + jnp.arange(node_rows, dtype=jnp.int32)
    has_upper = (global_rows > 0)[:, None]
    has_lower = (global_rows < tile_count * node_rows - 1)[:, None]
    section = lax.axis_index("pair")
    has_before = section > 0
    has_after = section < pair_count - 1
    weights = mobility[:, None]

    def relax(counter, carried):
        shifted, velocity = carried
        padded = extended(shifted.astype(jnp.bfloat16), (("tile", 2), ("pair", 0)), 1).astype(
            shifted.dtype
        )
        upper_rows = padded[1:2, :, 0:node_rows, :]
        lower_rows = padded[1:2, :, 2:, :]
        before = padded[0:1, :, 1:-1, :]
        following = padded[2:3, :, 1:-1, :]
        leftward = jnp.concatenate([shifted[..., :1], shifted[..., :-1]], axis=3)
        rightward = jnp.concatenate([shifted[..., 1:], shifted[..., -1:]], axis=3)
        laplace = (
            jnp.where(has_upper, upper_rows - shifted, 0.0)
            + jnp.where(has_lower, lower_rows - shifted, 0.0)
            + (leftward - shifted)
            + (rightward - shifted)
        )
        coupling = jnp.where(has_before, before - shifted, 0.0) + jnp.where(
            has_after, following - shifted, 0.0
        )
        forces = 0.35 * laplace + 0.2 * coupling + 0.3 * (target - shifted)
        velocity = 0.8 * velocity + weights * forces
        return (shifted + velocity, velocity)

    settled, last_velocity = lax.fori_loop(
        0, STEPS, relax, (prior_flow, jnp.zeros_like(prior_flow))
    )
    return (patch_flow, settled)


def solution(mesh):
    in_specs = (
        P("pair", "tile", None),
        P("pair", "tile", None, None),
        P("pair", "tile"),
        P("pair", "tile", None),
        P("pair", "tile", None),
        P("pair", None, "tile", None),
    )
    out_specs = (P("pair", None, "tile"), P("pair", None, "tile", None))
    return jax.shard_map(shards, mesh=mesh, in_specs=in_specs, out_specs=out_specs, check_vma=False)
```

profile of v0, /device:TPU:14, one launch (start us, length us, event | category | flops | bytes accessed | tf_op | source)
XLA Modules:
  0.0 1078.0 jit_solution(457253441389791129)
XLA Ops:
  7.0 12.1 %all-to-all-start = ((s32[64,2,3]{2,1,0:T(2,128)}), s32[64,2,3]{2,1,0:T(2,128)S(1)}, u32[]{:S(2)}, u32[]{:S(2)}) async-start(s32[64,2,3]{2,1,0:T(2,128)} %copy.114), calls=%async_computation | async-start | bytes 131072 | tf_op jit(solution)/shard_map/all_to_all | solution.py:142
  19.5 7.3 gather_fusion.2
  26.7 10.3 select_select_fusion
  37.1 10.5 all-to-all-start.1
  49.3 235.7 %while.31 = (s32[]{:T(128)}, bf16[512,512]{1,0:T(8,128)(2,1)}, s32[64,2]{0,1:T(2,128)S(1)}, bf16[64,160,160]{1,2,0:T(8,128)(2,1)}, s32[]{:T(128)}) while((s32[]{:T(128)}, bf16[512,512]{1,0:T(8,128)(2,1)}, s32[64,2]{0,1:T(2,128)S(1)}, bf16[64,160,160]{1,2,0:T(8,128)(2,1)}, s32[]{:T(128)}) %tuple.119), condition=%wide.while_cond.1, body=%wide.while_body.1.sunk | while | flops 2 | bytes 338537 | solution.py:98
  285.5 7.2 gather_fusion.3
  292.7 8.2 copy.121
  300.8 5.4 broadcast_select_fusion
  306.2 198.5 %while.32 = (s32[]{:T(128)}, f32[8,8,2]{1,2,0:T(2,128)S(1)}, bf16[8,8,160,160]{2,3,1,0:T(8,128)(2,1)}, bf16[8,8,160,160]{2,3,1,0:T(8,128)(2,1)}, s32[]{:T(128)}) while((s32[]{:T(128)}, f32[8,8,2]{1,2,0:T(2,128)S(1)}, bf16[8,8,160,160]{2,3,1,0:T(8,128)(2,1)}, bf16[8,8,160,160]{2,3,1,0:T(8,128)(2,1)}, s32[]{:T(128)}) %tuple.117), condition=%wide.region_9.10_spmd.clone.clone, body=%wide.region_5.9_spmd.clone.clone.sunk | while | flops 1192295040 | bytes 27203164 | solution.py:88
  506.3 10.4 all-to-all-start.2
  516.8 8.8 all-to-all-done.2
  526.9 549.3 %while.33 = (s32[]{:T(128)}, f32[1,2,16,512]{3,2,1,0:T(8,128)S(1)}, f32[1,2,16,512]{3,2,1,0:T(8,128)S(1)}, f32[1,1,16,512]{3,2,1,0:T(8,128)S(1)}, pred[]{:T(512)...) while((s32[]{:T(128)}, f32[1,2,16,512]{3,2,1,0:T(8,128)S(1)}, ...), condition=%wide.region_11.12_spmd.clone.clone.clone, body=%wide.region_10.11_spmd.clone.clone.clone.sunk | while | flops 1224755 | bytes 1356117 | solution.py:208
  532.0 5.0 collective-permute-done.1
  550.4 4.5 collective-permute-done.1
  568.1 4.5 collective-permute-done.1
  585.5 4.5 collective-permute-done.1
  602.6 4.5 collective-permute-done.1
  619.6 4.5 collective-permute-done.1
  653.8 4.5 collective-permute-done.1
  670.9 4.5 collective-permute-done.1
  687.9 4.5 collective-permute-done.1
  705.0 4.5 collective-permute-done.1
  739.2 4.5 collective-permute-done.1
  773.3 4.5 collective-permute-done.1
  (1029 shorter events, 938.7 us)
Async XLA Ops:
  7.0 30.1 %all-to-all-start = ((s32[64,2,3]{2,1,0:T(2,128)}), s32[64,2,3]{2,1,0:T(2,128)S(1)}, u32[]{:S(2)}, u32[]{:S(2)}) async-start(s32[64,2,3]{2,1,0:T(2,128)} %copy.114), calls=%async_computation | async-start | bytes 131072 | tf_op jit(solution)/shard_map/all_to_all | solution.py:142
  37.1 248.4 %all-to-all-start.1 = ((bf16[64,2,160,160]{3,2,1,0:T(8,128)(2,1)}), bf16[64,2,160,160]{3,2,1,0:T(8,128)(2,1)}, u32[]{:S(2)}, u32[]{:S(2)}) async-start(bf16[64,2,160,160]{3,2,1,0:T(8,128)(2,1)} %select_select_fusion), calls=%async_computation.1 | async-start | bytes 20971520 | tf_op jit(solution)/shard_map/all_to_all | solution.py:135
  506.3 19.2 %all-to-all-start.2 = ((f32[64,2,2]{2,1,0:T(2,128)}), f32[64,2,2]{2,1,0:T(2,128)S(1)}, u32[]{:S(2)}, u32[]{:S(2)}) async-start(f32[64,2,2]{2,1,0:T(2,128)} %select_select_fusion.1), calls=%async_computation.2 | async-start | bytes 131072 | tf_op jit(solution)/shard_map/all_to_all | solution.py:161
  529.9 7.0 collective-permute-start.1
  547.8 7.0 collective-permute-start.1
  565.5 7.0 collective-permute-start.1
  582.9 7.0 collective-permute-start.1
  600.0 7.0 collective-permute-start.1
  617.1 7.0 collective-permute-start.1
  634.1 7.0 collective-permute-start.1
  651.2 7.0 collective-permute-start.1
  668.3 7.0 collective-permute-start.1
  685.4 7.0 collective-permute-start.1
  702.4 7.0 collective-permute-start.1
  736.6 7.0 collective-permute-start.1
  770.8 7.0 collective-permute-start.1
  804.9 7.0 collective-permute-start.1
  856.1 7.0 collective-permute-start.1
  890.3 7.0 collective-permute-start.1
  924.5 7.0 collective-permute-start.1
  941.5 7.0 collective-permute-start.1
  975.7 7.0 collective-permute-start.1
  1009.8 7.0 collective-permute-start.1
  1061.1 7.0 collective-permute-start.1
  (121 other events, 611.1 us)
where the time goes:
time: 1090 us; the launch traced here: 1080 us
  waiting for transfers between devices  301 us (28%)
  starting transfers between devices  277 us (25%)
  local copies, waits for them, and re-layouts  272 us (25%)
  matrix products  197 us (18%)
  other arithmetic  25.3 us (2%)
    ppermute x64, waiting for transfers between devices, extended(): before = lax.ppermute(last, axis, up)  279 us
    gather x320, local copies, waits for them, and re-layouts  235 us
    ppermute x64, starting transfers between devices, extended(): after = lax.ppermute(leading, axis, down)  126 us
    ppermute x64, starting transfers between devices, extended(): before = lax.ppermute(last, axis, up)  118 us
    dot_general x80, matrix products, right_mul(): jnp.einsum('nab,bc->nac', batch, table, preferred_element_type=jnp.float32)  108 us
    dot_general x48, matrix products, left_mul(): jnp.einsum('ab,nbc->nac', table, batch, preferred_element_type=jnp.float32)  89.4 us
  transfers between devices with their start and end apart: 131, of which 97 were waited for; matrix products, arithmetic and copies ran while one was open for 24% of the time, Pallas kernels for 0%

commit v1 on v0

v1 whole, which is shorter than its diff:
```python
import functools
import math

import jax
import jax.numpy as jnp
import ml_dtypes
import numpy as np
from jax import lax
from jax.experimental import pallas as pl
from jax.experimental.pallas import tpu as pltpu
from jax.sharding import PartitionSpec as P

MESH = pl.DeviceIdType.MESH
NY, NZ, NC, NP = 4, 8, 2, 4
TILES = NY * NZ * NC
W = 160
TILE = 512
PATCH_DEV = 32
STEPS = 32
EPS = 1e-06
ROWS = 16
COLS = 512
TILES_X = COLS // 128
HALO = 32
PAD = 8
SPAN = ROWS + 2 * HALO
HIGH = SPAN + 2 * PAD
HALF = W // 2 + 1
BLK = 88
FREQ = 2 * BLK
WIN_ROWS = 176
WIN_COLS = 384
MAX_SHIFT = 224
GROUP = 4
DEPTH = 2


def device_at(y, z, c):
    return {"tile": (y * NZ + z) * NC + c}


def my_place():
    t = lax.axis_index("tile")
    return t, t // (NZ * NC), (t // NC) % NZ, t % NC


def halo_targets(t, p):
    for dp in range(NP):
        for d in range(-2, 3):
            if dp or d:
                there = {"tile": (t + d + TILES) % TILES, "pair": (p + dp) % NP}
                yield dp, d, there


def remote(src, dst, send, recv, device):
    return pltpu.make_async_remote_copy(
        src_ref=src, dst_ref=dst, send_sem=send, recv_sem=recv, device_id=device, device_id_type=MESH
    )


def greet(devices):
    barrier = pltpu.get_barrier_semaphore()
    for device in devices:
        pl.semaphore_signal(barrier, inc=1, device_id=device, device_id_type=MESH)
    pl.semaphore_wait(barrier, len(devices))


def relax_block(target, u_in, u_out, vel, mob, mask_up, mask_dn, rows, tiles):
    here = pl.ds(rows, 8)
    up, dn = mask_up[here, :], mask_dn[here, :]
    lane = lax.broadcasted_iota(jnp.int32, (8, 128), 1)
    for comp in range(2):
        u = [[u_in[s, comp, n, here, :] for n in range(tiles)] for s in range(NP)]
        steps = [[u[s + 1][n] - u[s][n] for n in range(tiles)] for s in range(NP - 1)]
        for s in range(NP):
            turned = [pltpu.roll(u[s][n], 1, axis=1) for n in range(tiles)]
            left = []
            for n in range(tiles):
                if tiles > 1:
                    other = turned[n - 1] if n else u[s][0]
                    left.append(u[s][n] - jnp.where(lane == 0, other, turned[n]))
                else:
                    left.append(u[s][n] - turned[n])
            turned = [pltpu.roll(left[n], 127, axis=1) for n in range(tiles)]
            for n in range(tiles):
                right = turned[n]
                if tiles > 1:
                    right = jnp.where(lane == 127, turned[n + 1] if n + 1 < tiles else 0.0, right)
                above = u_in[s, comp, n, pl.ds(rows - 1, 8), :]
                below = u_in[s, comp, n, pl.ds(rows + 1, 8), :]
                lap = (below - u[s][n]) * dn - (u[s][n] - above) * up + (right - left[n])
                if s == 0:
                    inter = steps[0][n]
                elif s == NP - 1:
                    inter = -steps[s - 1][n]
                else:
                    inter = steps[s][n] - steps[s - 1][n]
                force = 0.35 * lap + 0.2 * inter + 0.3 * (target[s, comp, n, here, :] - u[s][n])
                speed = 0.8 * vel[s, comp, n, here, :] + mob(s, n, here) * force
                vel[s, comp, n, here, :] = speed
                u_out[s, comp, n, here, :] = u[s][n] + speed


def row_masks(t):
    row = t * ROWS - HALO - PAD + lax.broadcasted_iota(jnp.int32, (HIGH, 128), 0)
    return (row != 0).astype(jnp.float32), (row != TILES * ROWS - 1).astype(jnp.float32)


def gather_kernel(
    img, pat, meta, prior, mob, gi, gpl, gpr, gmeta, u_own, mob_band,
    pv, pr, own, net, uu, vel, mask_up, mask_dn,
    lsem, ysend, yrecv, zsend, zrecv, dsend, drecv, msend, mrecv, hsend, hrecv,
):
    t, y, z, c = my_place()
    p = lax.axis_index("pair")
    right_y, left_y = device_at((y + 1) % NY, z, c), device_at((y + NY - 1) % NY, z, c)
    right_z, left_z = device_at(y, (z + 1) % NZ, c), device_at(y, (z + NZ - 1) % NZ, c)
    across_y = device_at((y + 2) % NY, z, c)
    sibling = device_at(y, z, 1 - c)
    stage = pltpu.make_async_copy(pat, pv, lsem.at[0])
    stage.start()
    mine = z * NC + c
    keep = pltpu.make_async_copy(img, gi.at[mine], lsem.at[1])
    keep.start()
    halo = list(halo_targets(t, p))
    greet([right_y, left_y, across_y, right_z, left_z, sibling] + [device for _, _, device in halo])

    lo, hi = pl.ds(0, 16), pl.ds(16, 16)
    glo, ghi = pl.ds(0, 4), pl.ds(4, 4)
    left_part = pl.ds(0, 128)
    sent = []
    yr, yl = [], []

    def start(copy, into=None):
        copy.start()
        sent.append(copy)
        if into is not None:
            into.append(copy)
        return copy

    def y_left(which, first, side, device, slot):
        return remote(
            pat.at[which, :, left_part], gpl.at[first, which], ysend.at[side, slot], yrecv.at[side, slot], device
        )

    start(y_left(hi, y, 0, right_y, 0), yr)
    start(y_left(lo, y, 1, left_y, 0), yl)

    for n in range(TILES_X):
        columns = pl.ds(128 * n, 128)
        own[0:2, n] = prior[:, :, columns]
        own[2, n] = mob[:, columns]
    meshes = []
    for n, (dp, d, device) in enumerate(halo):
        rows = pl.ds(PAD + ROWS * (2 - d), ROWS)
        copy = remote(own, net.at[p, :, :, rows, :], hsend.at[n], hrecv.at[n], device)
        start(copy, meshes)

    half = TILE // 2
    zr, zl, dd = [], [], []
    for q in range(2):
        rs = pl.ds(q * half, half)
        start(remote(img.at[rs], gi.at[mine, rs], zsend.at[0, q], zrecv.at[0, q], right_z), zr)
        rs = pl.ds((1 - q) * half, half)
        start(remote(img.at[rs], gi.at[mine, rs], zsend.at[1, q], zrecv.at[1, q], left_z), zl)
    start(y_left(lo, y, 0, right_y, 1), yr)
    start(y_left(hi, y, 1, left_y, 1), yl)
    metas = []
    for n, device in enumerate((right_y, left_y, across_y)):
        start(remote(meta, gmeta.at[y], msend.at[n], mrecv.at[n], device), metas)
    start(remote(img, gi.at[mine], dsend.at[0], drecv.at[0], sibling), dd)

    stage.wait()
    for g in range(PATCH_DEV // 4):
        pr[g] = jnp.concatenate([pv[4 * g + q, :, 128:W] for q in range(4)], axis=1)
    pairs = []
    pairs.append(start(remote(pr.at[ghi], gpr.at[y, ghi], ysend.at[0, 3], yrecv.at[0, 3], right_y)))
    pairs.append(start(remote(pr.at[glo], gpr.at[y, glo], ysend.at[1, 3], yrecv.at[1, 3], left_y)))
    pairs.append(start(remote(pr.at[glo], gpr.at[y, glo], ysend.at[0, 4], yrecv.at[0, 4], right_y)))
    pairs.append(start(remote(pr.at[ghi], gpr.at[y, ghi], ysend.at[1, 4], yrecv.at[1, 4], left_y)))
    local = [
        pltpu.make_async_copy(pv.at[:, :, left_part], gpl.at[y], lsem.at[2]),
        pltpu.make_async_copy(pr, gpr.at[y], lsem.at[3]),
        pltpu.make_async_copy(meta, gmeta.at[y], lsem.at[4]),
    ]
    for copy in local:
        copy.start()

    def forward_z(k, q):
        for side, hops, device in ((0, NZ - k, right_z), (1, k, left_z)):
            slot = ((z + hops) % NZ) * NC + c
            part = q if side == 0 else 1 - q
            rs = pl.ds(part * half, half)
            line = zr if side == 0 else zl
            line[2 * (k - 1) + q].wait_recv()
            block = gi.at[slot, rs]
            if k < 3 or (k == 3 and q == 0):
                start(remote(block, block, zsend.at[side, 2 * k + q], zrecv.at[side, 2 * k + q], device), line)
            n = len(dd)
            start(remote(block, block, dsend.at[n], drecv.at[n], sibling), dd)

    mask_up[...], mask_dn[...] = row_masks(t)
    edge = jnp.zeros((PAD, 128), jnp.float32)
    for s in range(NP):
        for comp in range(3):
            for n in range(TILES_X):
                net[s, comp, n, 0:PAD, :] = edge
                net[s, comp, n, HIGH - PAD :, :] = edge
    middle = pl.ds(PAD + HALO, ROWS)

    def begin():
        for copy in meshes:
            copy.wait_recv()
        net[p, :, :, middle, :] = own[...]

        @pl.loop(0, HIGH // 8)
        def _(b):
            here = pl.ds(pl.multiple_of(b * 8, 8), 8)
            values = net[:, 0:2, :, here, :]
            uu[0, :, :, :, here, :] = values
            uu[1, :, :, :, here, :] = values
            vel[:, :, :, here, :] = jnp.zeros_like(values)

    def relax(first, count):
        edge = first // 8

        @pl.loop(first, first + count)
        def _(step):
            @pl.loop(PAD // 8 + edge, (HIGH - PAD) // 8 - edge)
            def _(b):
                relax_block(
                    net, uu.at[step % 2], uu.at[(step + 1) % 2], vel,
                    lambda s, n, here: net[s, 2, n, here, :], mask_up, mask_dn,
                    pl.multiple_of(b * 8, 8), TILES_X,
                )

    forward_z(1, 0)
    forward_z(1, 1)
    begin()
    relax(0, 4)
    forward_z(2, 0)
    relax(4, 4)
    yr[0].wait_recv()
    yl[0].wait_recv()
    pairs[0].wait_recv()
    pairs[1].wait_recv()
    before, after = (y + NY - 1) % NY, (y + 1) % NY
    far = []
    for side, first, which, groups, device in ((0, before, hi, ghi, right_y), (1, after, lo, glo, left_y)):
        block = gpl.at[first, which]
        start(remote(block, block, ysend.at[side, 2], yrecv.at[side, 2], device), far)
        block = gpr.at[first, groups]
        start(remote(block, block, ysend.at[side, 5], yrecv.at[side, 5], device), far)
    forward_z(2, 1)
    relax(8, 4)
    forward_z(3, 0)
    relax(12, 4)
    forward_z(3, 1)
    relax(16, 4)
    forward_z(4, 0)
    relax(20, 12)

    for n in range(TILES_X):
        moved = jnp.zeros((2, ROWS, 128), jnp.float32)
        for s in range(NP):
            moved = jnp.where(p == s, uu[0, s, :, n, middle, :], moved)
        u_own[:, :, 128 * n : 128 * n + 128] = moved
    lane = lax.broadcasted_iota(jnp.int32, (SPAN, 128), 1)
    for s in range(NP):
        parts = [net[s, 2, n, PAD : PAD + SPAN, :] for n in range(4)]
        low = jnp.where(lane < 32, pltpu.roll(parts[0], 32, axis=1), pltpu.roll(parts[1], 32, axis=1))
        top = jnp.where(lane < 96, pltpu.roll(parts[2], 96, axis=1), pltpu.roll(parts[3], 96, axis=1))
        mob_band[s] = jnp.where(lane < 64, low, top)

    for copy in yr[1:] + yl[1:] + pairs[2:] + far + metas + dd:
        copy.wait_recv()
    for copy in sent:
        copy.wait_send()
    for copy in local:
        copy.wait()
    keep.wait()


def flow_kernel(
    meta, gi, gpl, gpr, rows_tab, cols_tab, quads_tab, inv_left, inv_right, out,
    items, xbuf, mbuf, sum_e, sum_r, sems,
):
    _, y, _, _ = my_place()

    def note(n, count):
        h, j = n // PATCH_DEV, n % PATCH_DEV
        items[count] = n
        return count + (meta[h, 0, j] // (NZ * NC) == y).astype(jnp.int32)

    count = lax.fori_loop(0, NY * PATCH_DEV, note, jnp.int32(0))
    sum_e[...] = jnp.zeros_like(sum_e)
    sum_r[...] = jnp.zeros_like(sum_r)
    rounds = (count + GROUP - 1) // GROUP

    def item(step, g):
        n = items[jnp.minimum(step * GROUP + g, count - 1)]
        return n // PATCH_DEV, n % PATCH_DEV

    def place(h, j):
        first_row, first_col = meta[h, 1, j], meta[h, 2, j]
        row = jnp.minimum(first_row // 16 * 16, TILE - WIN_ROWS)
        col = jnp.where(first_col >= 128, 128, 0)
        return row, first_row - row, col, first_col - col

    def copies(step, slot, g):
        h, j = item(step, g)
        row, _, col, _ = place(h, j)
        window = gi.at[
            meta[h, 0, j] % (NZ * NC),
            pl.ds(pl.multiple_of(row, 16), WIN_ROWS),
            pl.ds(pl.multiple_of(col, 128), WIN_COLS),
        ]
        return (
            pltpu.make_async_copy(window, xbuf.at[slot, g], sems.at[slot, g, 0]),
            pltpu.make_async_copy(gpl.at[h, j], mbuf.at[slot, g, :, pl.ds(0, 128)], sems.at[slot, g, 1]),
            pltpu.make_async_copy(gpr.at[h, j // 4], mbuf.at[slot, g, :, pl.ds(128, 128)], sems.at[slot, g, 2]),
        )

    def fetch(step, slot):
        for g in range(GROUP):
            for copy in copies(step, slot, g):
                copy.start()

    def dot(a, b):
        return jnp.dot(a, b, preferred_element_type=jnp.float32)

    signed = lax.broadcasted_iota(jnp.int32, (W, 256), 0)
    signed = jnp.where(signed < W // 2, signed, signed - W).astype(jnp.float32)

    def work(step, slot):
        results = []
        for g in range(GROUP):
            h, j = item(step, g)
            _, row_shift, _, col_shift = place(h, j)
            cut = pl.ds(MAX_SHIFT - col_shift, WIN_COLS)
            columns = jnp.concatenate([cols_tab[0, cut, :], cols_tab[1, cut, :]], axis=1).astype(jnp.bfloat16)
            fixed = dot(xbuf[slot, g], columns).astype(jnp.bfloat16)
            fixed = dot(rows_tab[row_shift], fixed)
            moving = dot(mbuf[slot, g], quads_tab[j % 4]).astype(jnp.bfloat16)
            moving = dot(rows_tab[0, :, 0:W], moving)
            fcc, fcs, fsc, fss = fixed[:BLK, :128], fixed[:BLK, 128:], fixed[BLK:, :128], fixed[BLK:, 128:]
            mcc, mcs, msc, mss = moving[:BLK, :128], moving[:BLK, 128:], moving[BLK:, :128], moving[BLK:, 128:]
            ee = fcc * mcc + fss * mss + fcs * mcs + fsc * msc
            oo = fcc * mss + fss * mcc - fcs * msc - fsc * mcs
            eo = fcc * mcs - fcs * mcc + fsc * mss - fss * msc
            oe = fcc * msc - fsc * mcc + fcs * mss - fss * mcs
            cross = jnp.concatenate(
                [jnp.concatenate([ee, eo], axis=1), jnp.concatenate([oe, oo], axis=1)], axis=0
            ).astype(jnp.bfloat16)
            back = dot(inv_left[...], cross).astype(jnp.bfloat16)
            corr = dot(back, inv_right[...])
            energy = corr * corr
            at = h * PATCH_DEV + j % 2 * ROWS + j // 2
            results.append(
                (at, jnp.sum(energy, axis=0, keepdims=True), jnp.sum(energy * signed, axis=0, keepdims=True))
            )
        for at, plain, by_row in results:
            sum_e[pl.ds(at, 1), :] = plain
            sum_r[pl.ds(at, 1), :] = by_row

    @pl.when(rounds > 0)
    def _():
        fetch(0, 0)

    def one(step, carry):
        slot = step % DEPTH

        @pl.when(step + 1 < rounds)
        def _():
            fetch(step + 1, (step + 1) % DEPTH)

        for g in range(GROUP):
            for copy in copies(step, slot, g):
                copy.wait()
        work(step, slot)
        return carry

    lax.fori_loop(0, rounds, one, 0)

    number = lax.broadcasted_iota(jnp.int32, (NY * PATCH_DEV, 256), 1)
    shift = jnp.where(number < W // 2, number, number - W).astype(jnp.float32)
    plain = sum_e[...]
    total = jnp.sum(plain, axis=1, keepdims=True) + EPS
    flows = (
        jnp.sum(sum_r[...], axis=1, keepdims=True) / total,
        jnp.sum(plain * shift, axis=1, keepdims=True) / total,
    )
    lane = lax.broadcasted_iota(jnp.int32, (ROWS, 128), 1)
    for h in range(NY):
        block = jnp.zeros((ROWS, 128), jnp.float32)
        for comp in range(2):
            for side in range(2):
                first = h * PATCH_DEV + side * ROWS
                block = jnp.where(lane == 32 + 64 * side + comp, flows[comp][first : first + ROWS], block)
        out[h] = block


def share_kernel(ep, net, got, total, fsend, frecv, hsend, hrecv, lsem):
    t, y, z, c = my_place()
    p = lax.axis_index("pair")
    homes = [device_at((y + d) % NY, z, c) for d in range(1, NY)]
    halo = list(halo_targets(t, p))
    greet(homes + [device for _, _, device in halo])
    first = []
    for n, device in enumerate(homes):
        copy = remote(ep.at[(y + n + 1) % NY], got.at[n], fsend.at[n], frecv.at[n], device)
        copy.start()
        first.append(copy)
    for copy in first:
        copy.wait_recv()
    total[...] = ep[y] + got[0] + got[1] + got[2]
    second = []
    for n, (dp, d, device) in enumerate(halo):
        copy = remote(total, net.at[p, pl.ds(ROWS * (2 - d), ROWS), :], hsend.at[n], hrecv.at[n], device)
        copy.start()
        second.append(copy)
    own = pltpu.make_async_copy(total, net.at[p, pl.ds(HALO, ROWS), :], lsem)
    own.start()
    for copy in second:
        copy.wait_recv()
    for copy in first + second:
        copy.wait_send()
    own.wait()


def settle_kernel(net, mob_band, u_own, flow, out, tgt, mob, ua, ub, vel, mask_up, mask_dn):
    t = lax.axis_index("tile")
    p = lax.axis_index("pair")
    mask_up[...], mask_dn[...] = row_masks(t)
    lane = lax.broadcasted_iota(jnp.int32, (SPAN, 128), 1)
    node = (lane == 32) | (lane == 96)
    edge = jnp.zeros((PAD, 128), jnp.float32)
    span = pl.ds(PAD, SPAN)
    vel[...] = jnp.zeros_like(vel)
    ua[...] = jnp.zeros_like(ua)
    ub[...] = jnp.zeros_like(ub)
    for s in range(NP):
        values = net[s]
        for comp in range(2):
            turned = values if comp == 0 else pltpu.roll(values, 127, axis=1)
            tgt[s, comp, 0, span, :] = jnp.where(node, turned, 0.0)
        mob[s, span, :] = mob_band[s]
        mob[s, 0:PAD, :] = edge
        mob[s, HIGH - PAD :, :] = edge

    for first in range(0, STEPS, 8):

        @pl.loop(0, 4)
        def _(_):
            for u_in, u_out in ((ua, ub), (ub, ua)):
                for rows in range(PAD + first, HIGH - PAD - first, 8):
                    relax_block(
                        tgt, u_in, u_out, vel, lambda s, n, here: mob[s, here, :], mask_up, mask_dn, rows, 1
                    )

    middle = pl.ds(PAD + HALO, ROWS)
    lane = lax.broadcasted_iota(jnp.int32, (ROWS, 128), 1)
    row = lax.broadcasted_iota(jnp.int32, (ROWS, 128), 0)
    for comp in range(2):
        moved = jnp.zeros((ROWS, 128), jnp.float32)
        given = jnp.zeros((ROWS, 128), jnp.float32)
        for s in range(NP):
            moved = jnp.where(p == s, ua[s, comp, 0, middle, :], moved)
            given = jnp.where(p == s, tgt[s, comp, 0, middle, :], given)
        wide, narrow = pltpu.roll(moved, 96, axis=1), pltpu.roll(moved, 32, axis=1)
        for n, (part, inside) in enumerate(((wide, lane >= 96), (wide, lane < 32), (narrow, lane >= 96), (narrow, lane < 32))):
            columns = pl.ds(128 * n, 128)
            out[comp, :, columns] = u_own[comp, :, columns] + jnp.where(inside, part, 0.0)
        even = jnp.sum(jnp.where(lane == 32, given, 0.0), axis=1, keepdims=True)
        odd = jnp.sum(jnp.where(lane == 96, given, 0.0), axis=1, keepdims=True)
        spread = jnp.where(lane == 2 * row, even, 0.0) + jnp.where(lane == 2 * row + 1, odd, 0.0)
        flow[comp : comp + 1, :] = jnp.sum(spread, axis=0, keepdims=True)[:, :PATCH_DEV]


def make_tables():
    numbers = np.arange(W)
    phase = (numbers[:, None] * numbers[None, :] % W).astype(np.float32) * np.float32(2.0 * math.pi / W)
    scale = np.float32(1.0 / math.sqrt(W))
    cos = (np.cos(phase) * scale).astype(ml_dtypes.bfloat16).astype(np.float32)
    sin = (np.sin(phase) * scale).astype(ml_dtypes.bfloat16).astype(np.float32)
    left = np.zeros((FREQ, W), np.float32)
    left[:HALF], left[BLK : BLK + HALF] = cos[:HALF], sin[:HALF]
    right = np.zeros((W, 256), np.float32)
    right[:, :HALF], right[:, 128 : 128 + HALF] = cos[:, :HALF], sin[:, :HALF]
    rows_tab = np.zeros((17, FREQ, WIN_ROWS), np.float32)
    for shift in range(17):
        rows_tab[shift, :, shift : shift + W] = left
    cols_tab = np.zeros((2, MAX_SHIFT + WIN_COLS, 128), np.float32)
    cols_tab[0, MAX_SHIFT : MAX_SHIFT + W] = right[:, :128]
    cols_tab[1, MAX_SHIFT : MAX_SHIFT + W] = right[:, 128:]
    quads_tab = np.zeros((4, 256, 256), np.float32)
    for q in range(4):
        quads_tab[q, :128] = right[:128]
        quads_tab[q, 128 + 32 * q : 160 + 32 * q] = right[128:]
    weight = np.full((HALF, 1), 2.0, np.float32)
    weight[0] = weight[-1] = 1.0
    inv_left = np.zeros((W, FREQ), np.float32)
    inv_left[:, :HALF], inv_left[:, BLK : BLK + HALF] = (weight * cos[:HALF]).T, (-2.0 * sin[:HALF]).T
    inv_right = np.zeros((256, 256), np.float32)
    inv_right[:HALF, :W], inv_right[128 : 128 + HALF, :W] = weight * cos[:HALF], -2.0 * sin[:HALF]
    half = lambda table: table.astype(ml_dtypes.bfloat16)
    return half(rows_tab), cols_tab, half(quads_tab), half(inv_left), half(inv_right)


def any_spec():
    return pl.BlockSpec(memory_space=pl.ANY)


def vmem_spec():
    return pl.BlockSpec(memory_space=pltpu.VMEM)


def shards(fixed_image, moving_patches, owners, offsets, mobility, prior_flow):
    meta = jnp.pad(jnp.concatenate([owners, offsets[0].T], axis=0), ((0, 5), (0, 96)))
    f32, bf16 = jnp.float32, jnp.bfloat16
    sds = jax.ShapeDtypeStruct
    dma = pltpu.SemaphoreType.DMA
    gi, gpl, gpr, gmeta, u_own, mob_band = pl.pallas_call(
        gather_kernel,
        out_shape=(
            sds((NZ * NC, TILE, TILE), bf16),
            sds((NY, PATCH_DEV, W, 128), bf16),
            sds((NY, PATCH_DEV // 4, W, 128), bf16),
            sds((NY, 8, 128), jnp.int32),
            sds((2, ROWS, COLS), f32),
            sds((NP, SPAN, 128), f32),
        ),
        in_specs=[any_spec(), any_spec(), vmem_spec(), vmem_spec(), vmem_spec()],
        out_specs=(any_spec(), any_spec(), any_spec(), any_spec(), vmem_spec(), vmem_spec()),
        scratch_shapes=[
            pltpu.VMEM((PATCH_DEV, W, W), bf16),
            pltpu.VMEM((PATCH_DEV // 4, W, 128), bf16),
            pltpu.VMEM((3, TILES_X, ROWS, 128), f32),
            pltpu.VMEM((NP, 3, TILES_X, HIGH, 128), f32),
            pltpu.VMEM((2, NP, 2, TILES_X, HIGH, 128), f32),
            pltpu.VMEM((NP, 2, TILES_X, HIGH, 128), f32),
            pltpu.VMEM((HIGH, 128), f32),
            pltpu.VMEM((HIGH, 128), f32),
            dma((5,)), dma((2, 6)), dma((2, 6)), dma((2, 8)), dma((2, 8)), dma((16,)), dma((16,)),
            dma((3,)), dma((3,)), dma((19,)), dma((19,)),
        ],
        compiler_params=pltpu.CompilerParams(
            collective_id=0, has_side_effects=True, vmem_limit_bytes=32 * 2**20
        ),
        name="gather_and_relax",
    )(fixed_image[0], moving_patches[0], meta, prior_flow[0], mobility[0])
    tables = [jnp.asarray(table) for table in make_tables()]
    ep = pl.pallas_call(
        flow_kernel,
        out_shape=sds((NY, ROWS, 128), f32),
        in_specs=[pl.BlockSpec(memory_space=pltpu.SMEM)] + [any_spec()] * 3 + [vmem_spec()] * 5,
        out_specs=vmem_spec(),
        scratch_shapes=[
            pltpu.SMEM((NY * PATCH_DEV + 1,), jnp.int32),
            pltpu.VMEM((DEPTH, GROUP, WIN_ROWS, WIN_COLS), bf16),
            pltpu.VMEM((DEPTH, GROUP, W, 256), bf16),
            pltpu.VMEM((NY * PATCH_DEV, 256), f32),
            pltpu.VMEM((NY * PATCH_DEV, 256), f32),
            dma((DEPTH, GROUP, 3)),
        ],
        compiler_params=pltpu.CompilerParams(vmem_limit_bytes=32 * 2**20),
        name="patch_flows",
    )(gmeta, gi, gpl, gpr, *tables)
    net = pl.pallas_call(
        share_kernel,
        out_shape=sds((NP, SPAN, 128), f32),
        in_specs=[vmem_spec()],
        out_specs=any_spec(),
        scratch_shapes=[
            pltpu.VMEM((3, ROWS, 128), f32), pltpu.VMEM((ROWS, 128), f32),
            dma((3,)), dma((3,)), dma((19,)), dma((19,)), dma(()),
        ],
        compiler_params=pltpu.CompilerParams(collective_id=1, has_side_effects=True),
        name="share_flows",
    )(ep)
    flow, out = pl.pallas_call(
        settle_kernel,
        out_shape=(sds((2, PATCH_DEV), f32), sds((2, ROWS, COLS), f32)),
        in_specs=[vmem_spec()] * 3,
        out_specs=(vmem_spec(), vmem_spec()),
        scratch_shapes=[
            pltpu.VMEM((NP, 2, 1, HIGH, 128), f32),
            pltpu.VMEM((NP, HIGH, 128), f32),
            pltpu.VMEM((NP, 2, 1, HIGH, 128), f32),
            pltpu.VMEM((NP, 2, 1, HIGH, 128), f32),
            pltpu.VMEM((NP, 2, 1, HIGH, 128), f32),
            pltpu.VMEM((HIGH, 128), f32),
            pltpu.VMEM((HIGH, 128), f32),
        ],
        compiler_params=pltpu.CompilerParams(vmem_limit_bytes=32 * 2**20),
        name="settle",
    )(net, mob_band, u_own)
    return flow[None], out[None]


def solution(mesh):
    in_specs = (
        P("pair", "tile", None),
        P("pair", "tile", None, None),
        P("pair", "tile"),
        P("pair", "tile", None),
        P("pair", "tile", None),
        P("pair", None, "tile", None),
    )
    out_specs = (P("pair", None, "tile"), P("pair", None, "tile", None))
    return jax.shard_map(shards, mesh=mesh, in_specs=in_specs, out_specs=out_specs, check_vma=False)
```

time: 1090 us -> 303 us (0.28)
  the two profiles are of different devices: /device:TPU:14 before, /device:TPU:1 now
where the time goes in v1:
time: 303 us; the launch traced here: 302 us
  Pallas kernels  295 us (97%)
  local copies, waits for them, and re-layouts  5.92 us (2%)
    pallas_call x1, Pallas kernels, shards(): pl.pallas_call(gather_kernel, out_shape=(sds((NZ * NC, TILE, TILE), bf16)...  236 us
    pallas_call x1, Pallas kernels, shards(): pl.pallas_call(flow_kernel, out_shape=sds((NY, ROWS, 128), f32), in_specs...  29.5 us
    pallas_call x1, Pallas kernels, shards(): pl.pallas_call(share_kernel, out_shape=sds((NP, SPAN, 128), f32), in_spec...  19.3 us
    pallas_call x1, Pallas kernels, shards(): pl.pallas_call(settle_kernel, out_shape=(sds((2, PATCH_DEV), f32), sds((2...  10.2 us

profile of v1, /device:TPU:1, one launch (start us, length us, event | category | flops | bytes accessed | tf_op | source)
XLA Modules:
  0.0 302.2 jit_solution(13062106811084899823)
XLA Ops:
  0.6 0.7 pad_add_fusion
  1.3 0.0 copy-start
  1.3 1.7 copy-done
  3.1 0.0 copy-start.4
  3.1 1.0 copy-done.4
  4.1 0.0 copy-start.9
  4.1 0.8 copy-done.9
  5.0 0.0 copy-start.10
  5.0 0.8 copy-done.10
  5.7 0.0 copy-start.1
  5.7 0.0 copy-start.8
  5.7 235.8 %gather_and_relax.1 = (bf16[16,512,512]{2,1,0:T(8,128)(2,1)S(1)}, bf16[4,32,160,128]{3,2,1,0:T(8,128)(2,1)S(1)}, bf16[4,8,160,128]{3,2,1,0:T(8,128)(2,1)S(1)}, s...) custom-call(bf16[512,512]{1,0:T(8,128)(2,1)S(1)} %bitcast.10, ...), custom_call_target="tpu_custom_call" | custom-call | tf_op jit(solution)/shard_map/gather_and_relax/pallas_call | solution.py:523
  241.6 0.0 copy-done.1
  241.6 0.0 copy-done.3
  241.6 0.0 copy-done.5
  241.6 0.0 copy-done.6
  241.6 0.0 copy-done.8
  241.6 29.5 %patch_flows.1.ep = f32[4,16,128]{2,1,0:T(8,128)S(1)} custom-call(s32[4,8,128]{2,1,0:T(8,128)S(1)} %get-tuple-element.10.meta, bf16[16,512,512]{2,1,0:T(8,128)(2,1)S(1)} %get-tuple-element.11.gi, bf16[4,32,160,128]{3,2,1,0:T(8,128)(2,1)S(1)} %get-tuple-element.12.gpl, bf16[4,8,160,128]{3,2,1,0:T(8,128)(2,1)S(1)} %get-tuple-element.13.gpr, ...), custom_call_target="tpu_custom_call" | custom-call | tf_op jit(solution)/shard_map/patch_flows/pallas_call | solution.py:553
  271.1 0.0 copy-start.7
  271.1 0.6 copy-done.7
  271.8 19.3 %share_flows.1.net = f32[4,80,128]{2,1,0:T(8,128)} custom-call(f32[4,16,128]{2,1,0:T(8,128)} %copy-done.7), custom_call_target="tpu_custom_call" | custom-call | tf_op jit(solution)/shard_map/share_flows/pallas_call | solution.py:569
  291.1 0.0 copy-start.2
  291.1 0.9 copy-done.2
  292.0 10.2 %settle.1 = (f32[2,32]{1,0:T(2,128)}, f32[2,16,512]{2,1,0:T(8,128)}) custom-call(f32[4,80,128]{2,1,0:T(8,128)S(1)} %copy-done.2, f32[4,80,128]{2,1,0:T(8,128)S(1)} %get-tuple-element.14.mob_band, f32[2,16,512]{2,1,0:T(8,128)S(1)} %get-tuple-element.15.u_own), custom_call_target="tpu_custom_call" | custom-call | tf_op jit(solution)/shard_map/settle/pallas_call | solution.py:581
  (4 shorter events, 0.0 us)
Async XLA Ops:
  1.3 1.7 copy-start
  3.1 1.0 copy-start.4
  4.1 0.8 copy-start.9
  5.0 0.8 copy-start.10
  5.7 235.9 %copy-start.1 = (bf16[17,176,176]{2,1,0:T(8,128)(2,1)S(1)}, bf16[17,176,176]{2,1,0:T(8,128)(2,1)}, u32[]{:S(2)}) copy-start(bf16[17,176,176]{2,1,0:T(8,128)(2,1)} %constant.12.clone.rows_tab) | copy-start | bytes 3159556
  5.7 235.9 %copy-start.3 = (f32[2,608,128]{2,1,0:T(8,128)S(1)}, f32[2,608,128]{2,1,0:T(8,128)}, u32[]{:S(2)}) copy-start(f32[2,608,128]{2,1,0:T(8,128)} %constant.13.clone.cols_tab) | copy-start | bytes 1867780
  5.7 235.9 %copy-start.5 = (bf16[4,256,256]{2,1,0:T(8,128)(2,1)S(1)}, bf16[4,256,256]{2,1,0:T(8,128)(2,1)}, u32[]{:S(2)}) copy-start(bf16[4,256,256]{2,1,0:T(8,128)(2,1)} %constant.14.clone.quads_tab) | copy-start | bytes 1572868
  5.7 235.9 %copy-start.6 = (bf16[256,256]{1,0:T(8,128)(2,1)S(1)}, bf16[256,256]{1,0:T(8,128)(2,1)}, u32[]{:S(2)}) copy-start(bf16[256,256]{1,0:T(8,128)(2,1)} %constant.16.clone.inv_right) | copy-start | bytes 393220
  5.7 235.9 %copy-start.8 = (bf16[160,176]{1,0:T(8,128)(2,1)S(1)}, bf16[160,176]{1,0:T(8,128)(2,1)}, u32[]{:S(2)}) copy-start(bf16[160,176]{1,0:T(8,128)(2,1)} %constant.15.clone.inv_left) | copy-start | bytes 168964
  271.1 0.6 copy-start.7
  291.1 0.9 copy-start.2

commit v2 on v1

--- a/solution.py
+++ b/solution.py
@@ -30,8 +30,7 @@
 FREQ = 2 * BLK
 WIN_ROWS = 176
 WIN_COLS = 384
-MAX_SHIFT = 224
-GROUP = 4
+GROUP = 8
 DEPTH = 2
 
 
@@ -65,50 +64,36 @@
     pl.semaphore_wait(barrier, len(devices))
 
 
-def relax_block(target, u_in, u_out, vel, mob, mask_up, mask_dn, rows, tiles):
-    here = pl.ds(rows, 8)
-    up, dn = mask_up[here, :], mask_dn[here, :]
-    lane = lax.broadcasted_iota(jnp.int32, (8, 128), 1)
-    for comp in range(2):
-        u = [[u_in[s, comp, n, here, :] for n in range(tiles)] for s in range(NP)]
-        steps = [[u[s + 1][n] - u[s][n] for n in range(tiles)] for s in range(NP - 1)]
-        for s in range(NP):
-            turned = [pltpu.roll(u[s][n], 1, axis=1) for n in range(tiles)]
-            left = []
-            for n in range(tiles):
-                if tiles > 1:
-                    other = turned[n - 1] if n else u[s][0]
-                    left.append(u[s][n] - jnp.where(lane == 0, other, turned[n]))
-                else:
-                    left.append(u[s][n] - turned[n])
-            turned = [pltpu.roll(left[n], 127, axis=1) for n in range(tiles)]
-            for n in range(tiles):
-                right = turned[n]
-                if tiles > 1:
-                    right = jnp.where(lane == 127, turned[n + 1] if n + 1 < tiles else 0.0, right)
-                above = u_in[s, comp, n, pl.ds(rows - 1, 8), :]
-                below = u_in[s, comp, n, pl.ds(rows + 1, 8), :]
-                lap = (below - u[s][n]) * dn - (u[s][n] - above) * up + (right - left[n])
-                if s == 0:
-                    inter = steps[0][n]
-                elif s == NP - 1:
-                    inter = -steps[s - 1][n]
-                else:
-                    inter = steps[s][n] - steps[s - 1][n]
-                force = 0.35 * lap + 0.2 * inter + 0.3 * (target[s, comp, n, here, :] - u[s][n])
-                speed = 0.8 * vel[s, comp, n, here, :] + mob(s, n, here) * force
-                vel[s, comp, n, here, :] = speed
-                u_out[s, comp, n, here, :] = u[s][n] + speed
-
-
-def row_masks(t):
-    row = t * ROWS - HALO - PAD + lax.broadcasted_iota(jnp.int32, (HIGH, 128), 0)
-    return (row != 0).astype(jnp.float32), (row != TILES * ROWS - 1).astype(jnp.float32)
+def relax_step(t, target, u_in, u_out, vel, mob, first, last, tiles):
+    shape = (NP, tiles, 8, 128)
+    lane = lax.broadcasted_iota(jnp.int32, shape, 3)
+    line = lax.broadcasted_iota(jnp.int32, shape, 2)
+    own = PAD + HALO
+    for rows in range(first, last, 8):
+        here = pl.ds(rows, 8)
+        for comp in range(2):
+            u = u_in[:, comp, :, here, :]
+            above = u_in[:, comp, :, pl.ds(rows - 1, 8), :]
+            below = u_in[:, comp, :, pl.ds(rows + 1, 8), :]
+            if rows in (own, own - ROWS):
+                above = jnp.where((line == 0) & (t == (own - rows) // ROWS), u, above)
+            if rows + 8 in (own + ROWS, own + 2 * ROWS):
+                below = jnp.where((line == 7) & (t == TILES - (rows + 8 - own) // ROWS), u, below)
+            left, right = pltpu.roll(u, 1, axis=3), pltpu.roll(u, 127, axis=3)
+            if tiles > 1:
+                left = jnp.where(lane == 0, jnp.concatenate([u[:, :1], left[:, :-1]], axis=1), left)
+                right = jnp.where(lane == 127, jnp.concatenate([right[:, 1:], u[:, -1:]], axis=1), right)
+            inter = jnp.concatenate([u[:1], u[:-1]], axis=0) + jnp.concatenate([u[1:], u[-1:]], axis=0)
+            force = ((above + below) + (left + right)) + (0.2 / 0.35) * inter
+            force = force + target[:, comp, :, here, :] - (4.0 + 0.7 / 0.35) * u
+            speed = 0.8 * vel[:, comp, :, here, :] + mob(here) * force
+            vel[:, comp, :, here, :] = speed
+            u_out[:, comp, :, here, :] = u + speed
 
 
 def gather_kernel(
     img, pat, meta, prior, mob, gi, gpl, gpr, gmeta, u_own, mob_band,
-    pv, pr, own, net, uu, vel, mask_up, mask_dn,
+    pv, pr, own, net, target, ua, ub, vel,
     lsem, ysend, yrecv, zsend, zrecv, dsend, drecv, msend, mrecv, hsend, hrecv,
 ):
     t, y, z, c = my_place()
@@ -148,11 +133,11 @@
 
     for n in range(TILES_X):
         columns = pl.ds(128 * n, 128)
-        own[0:2, n] = prior[:, :, columns]
-        own[2, n] = mob[:, columns]
+        own[0:2, n] = prior[:, :, columns].astype(jnp.bfloat16)
+        own[2, n] = mob[:, columns].astype(jnp.bfloat16)
     meshes = []
     for n, (dp, d, device) in enumerate(halo):
-        rows = pl.ds(PAD + ROWS * (2 - d), ROWS)
+        rows = pl.ds(ROWS * (2 - d), ROWS)
         copy = remote(own, net.at[p, :, :, rows, :], hsend.at[n], hrecv.at[n], device)
         start(copy, meshes)
 
@@ -199,47 +184,49 @@
             n = len(dd)
             start(remote(block, block, dsend.at[n], drecv.at[n], sibling), dd)
 
-    mask_up[...], mask_dn[...] = row_masks(t)
-    edge = jnp.zeros((PAD, 128), jnp.float32)
-    for s in range(NP):
-        for comp in range(3):
-            for n in range(TILES_X):
-                net[s, comp, n, 0:PAD, :] = edge
-                net[s, comp, n, HIGH - PAD :, :] = edge
     middle = pl.ds(PAD + HALO, ROWS)
 
     def begin():
         for copy in meshes:
             copy.wait_recv()
-        net[p, :, :, middle, :] = own[...]
-
-        @pl.loop(0, HIGH // 8)
-        def _(b):
-            here = pl.ds(pl.multiple_of(b * 8, 8), 8)
-            values = net[:, 0:2, :, here, :]
-            uu[0, :, :, :, here, :] = values
-            uu[1, :, :, :, here, :] = values
-            vel[:, :, :, here, :] = jnp.zeros_like(values)
-
-    def relax(first, count):
-        edge = first // 8
-
-        @pl.loop(first, first + count)
-        def _(step):
-            @pl.loop(PAD // 8 + edge, (HIGH - PAD) // 8 - edge)
-            def _(b):
-                relax_block(
-                    net, uu.at[step % 2], uu.at[(step + 1) % 2], vel,
-                    lambda s, n, here: net[s, 2, n, here, :], mask_up, mask_dn,
-                    pl.multiple_of(b * 8, 8), TILES_X,
+        net[p, :, :, HALO : HALO + ROWS, :] = own[...]
+        edge = jnp.zeros((NP, 2, TILES_X, PAD, 128), jnp.float32)
+        for ref in (ua, ub):
+            ref[:, :, :, 0:PAD, :] = edge
+            ref[:, :, :, HIGH - PAD :, :] = edge
+
+        @pl.loop(0, NP)
+        def _(s):
+            for b in range(SPAN // ROWS):
+                rows = pl.ds(PAD + ROWS * b, ROWS)
+                values = net[s, :, :, ROWS * b : ROWS * b + ROWS, :].astype(jnp.float32)
+                ua[s, :, :, rows, :] = values[0:2]
+                ub[s, :, :, rows, :] = values[0:2]
+                vel[s, :, :, rows, :] = jnp.zeros_like(values[0:2])
+                target[s, 0:2, :, rows, :] = (0.3 / 0.35) * values[0:2]
+                target[s, 2, :, rows, :] = 0.35 * values[2]
+
+        for n in range(TILES_X):
+            columns = pl.ds(128 * n, 128)
+            values = prior[:, :, columns]
+            ua[p, :, n, middle, :] = values
+            target[p, 0:2, n, middle, :] = (0.3 / 0.35) * values
+            target[p, 2, n, middle, :] = 0.35 * mob[:, columns]
+
+    def relax(first):
+        @pl.loop(0, 4)
+        def _(_):
+            for u_in, u_out in ((ua, ub), (ub, ua)):
+                relax_step(
+                    t, target, u_in, u_out, vel, lambda here: target[:, 2, :, here, :],
+                    PAD + first, HIGH - PAD - first, TILES_X,
                 )
 
     forward_z(1, 0)
     forward_z(1, 1)
     begin()
-    relax(0, 4)
+    relax(0)
     forward_z(2, 0)
-    relax(4, 4)
     yr[0].wait_recv()
     yl[0].wait_recv()
     pairs[0].wait_recv()
@@ -251,23 +238,22 @@
         start(remote(block, block, ysend.at[side, 2], yrecv.at[side, 2], device), far)
         block = gpr.at[first, groups]
         start(remote(block, block, ysend.at[side, 5], yrecv.at[side, 5], device), far)
+    relax(8)
     forward_z(2, 1)
-    relax(8, 4)
+    relax(16)
     forward_z(3, 0)
-    relax(12, 4)
+    relax(24)
     forward_z(3, 1)
-    relax(16, 4)
     forward_z(4, 0)
-    relax(20, 12)
 
     for n in range(TILES_X):
         moved = jnp.zeros((2, ROWS, 128), jnp.float32)
         for s in range(NP):
-            moved = jnp.where(p == s, uu[0, s, :, n, middle, :], moved)
+            moved = jnp.where(p == s, ua[s, :, n, middle, :], moved)
         u_own[:, :, 128 * n : 128 * n + 128] = moved
     lane = lax.broadcasted_iota(jnp.int32, (SPAN, 128), 1)
     for s in range(NP):
-        parts = [net[s, 2, n, PAD : PAD + SPAN, :] for n in range(4)]
+        parts = [target[s, 2, n, PAD : PAD + SPAN, :] for n in range(4)]
         low = jnp.where(lane < 32, pltpu.roll(parts[0], 32, axis=1), pltpu.roll(parts[1], 32, axis=1))
         top = jnp.where(lane < 96, pltpu.roll(parts[2], 96, axis=1), pltpu.roll(parts[3], 96, axis=1))
         mob_band[s] = jnp.where(lane < 64, low, top)
@@ -282,17 +268,24 @@
 
 
 def flow_kernel(
-    meta, gi, gpl, gpr, rows_tab, cols_tab, quads_tab, inv_left, inv_right, out,
-    items, xbuf, mbuf, sum_e, sum_r, sems,
+    meta, gi, gpl, gpr, rows_hbm, cols_hbm, left_hbm, right_hbm, out,
+    items, rows_tab, cols_tab, inv_left, inv_right, xbuf, mbuf, lines, halves, backs, sum_e, sum_r, sems, tsems,
 ):
     _, y, _, _ = my_place()
-
-    def note(n, count):
-        h, j = n // PATCH_DEV, n % PATCH_DEV
-        items[count] = n
-        return count + (meta[h, 0, j] // (NZ * NC) == y).astype(jnp.int32)
-
-    count = lax.fori_loop(0, NY * PATCH_DEV, note, jnp.int32(0))
+    tables = [
+        pltpu.make_async_copy(src, dst, tsems.at[n])
+        for n, (src, dst) in enumerate(
+            ((cols_hbm, cols_tab), (rows_hbm, rows_tab), (left_hbm, inv_left), (right_hbm, inv_right))
+        )
+    ]
+
+    def note(h, count):
+        for j in range(PATCH_DEV):
+            items[count] = h * PATCH_DEV + j
+            count = count + (meta[h, 0, j] // (NZ * NC) == y).astype(jnp.int32)
+        return count
+
+    count = lax.fori_loop(0, NY, note, jnp.int32(0))
     sum_e[...] = jnp.zeros_like(sum_e)
     sum_r[...] = jnp.zeros_like(sum_r)
     rounds = (count + GROUP - 1) // GROUP
@@ -304,22 +297,22 @@
     def place(h, j):
         first_row, first_col = meta[h, 1, j], meta[h, 2, j]
         row = jnp.minimum(first_row // 16 * 16, TILE - WIN_ROWS)
-        col = jnp.where(first_col >= 128, 128, 0)
+        col = first_col // 128 * 128
         return row, first_row - row, col, first_col - col
 
     def copies(step, slot, g):
         h, j = item(step, g)
         row, _, col, _ = place(h, j)
-        window = gi.at[
-            meta[h, 0, j] % (NZ * NC),
-            pl.ds(pl.multiple_of(row, 16), WIN_ROWS),
-            pl.ds(pl.multiple_of(col, 128), WIN_COLS),
-        ]
-        return (
-            pltpu.make_async_copy(window, xbuf.at[slot, g], sems.at[slot, g, 0]),
-            pltpu.make_async_copy(gpl.at[h, j], mbuf.at[slot, g, :, pl.ds(0, 128)], sems.at[slot, g, 1]),
-            pltpu.make_async_copy(gpr.at[h, j // 4], mbuf.at[slot, g, :, pl.ds(128, 128)], sems.at[slot, g, 2]),
+        image = gi.at[meta[h, 0, j] % (NZ * NC)]
+        rows = pl.ds(pl.multiple_of(row, 16), WIN_ROWS)
+        third = jnp.minimum(col + 256, TILE - 128)
+        pieces = (
+            (image.at[rows, pl.ds(pl.multiple_of(col, 128), 256)], xbuf.at[slot, g, :, pl.ds(0, 256)]),
+            (image.at[rows, pl.ds(pl.multiple_of(third, 128), 128)], xbuf.at[slot, g, :, pl.ds(256, 128)]),
+            (gpl.at[h, j], mbuf.at[slot, g, :, pl.ds(0, 128)]),
+            (gpr.at[h, j // 4], mbuf.at[slot, g, :, pl.ds(128, 128)]),
         )
+        return [pltpu.make_async_copy(src, dst, sems.at[slot, g, n]) for n, (src, dst) in enumerate(pieces)]
 
     def fetch(step, slot):
         for g in range(GROUP):
@@ -331,18 +324,37 @@
 
     signed = lax.broadcasted_iota(jnp.int32, (W, 256), 0)
     signed = jnp.where(signed < W // 2, signed, signed - W).astype(jnp.float32)
+    win_lane = lax.broadcasted_iota(jnp.int32, (WIN_ROWS, 128), 1)
+    base = GROUP * WIN_ROWS
+
+    def turn(x, amount):
+        return pltpu.roll(x.astype(jnp.float32), (128 - amount) % 128, axis=1)
 
     def work(step, slot):
-        results = []
+        place_of = []
         for g in range(GROUP):
             h, j = item(step, g)
             _, row_shift, _, col_shift = place(h, j)
-            cut = pl.ds(MAX_SHIFT - col_shift, WIN_COLS)
-            columns = jnp.concatenate([cols_tab[0, cut, :], cols_tab[1, cut, :]], axis=1).astype(jnp.bfloat16)
-            fixed = dot(xbuf[slot, g], columns).astype(jnp.bfloat16)
-            fixed = dot(rows_tab[row_shift], fixed)
-            moving = dot(mbuf[slot, g], quads_tab[j % 4]).astype(jnp.bfloat16)
-            moving = dot(rows_tab[0, :, 0:W], moving)
+            place_of.append((h, j, row_shift))
+            parts = [turn(xbuf[slot, g, :, 128 * n : 128 * n + 128], col_shift) for n in range(3)]
+            inside = win_lane < 128 - col_shift
+            rows = pl.ds(g * WIN_ROWS, WIN_ROWS)
+            lines[rows, 0:128] = jnp.where(inside, parts[0], parts[1]).astype(jnp.bfloat16)
+            lines[rows, 128:256] = jnp.where(inside, parts[1], parts[2]).astype(jnp.bfloat16)
+            rows = pl.ds(base + g * W, W)
+            lines[rows, 0:128] = mbuf[slot, g, :, 0:128]
+            lines[rows, 128:256] = turn(mbuf[slot, g, :, 128:256], j % 4 * 32).astype(jnp.bfloat16)
+        halves[...] = dot(lines[...], cols_tab[...]).astype(jnp.bfloat16)
+        spectra = [
+            (
+                dot(rows_tab[place_of[g][2]], halves[pl.ds(g * WIN_ROWS, WIN_ROWS), :]),
+                dot(rows_tab[0, :, 0:W], halves[pl.ds(base + g * W, W), :]),
+            )
+            for g in range(GROUP)
+        ]
+        crosses = []
+        for g in range(GROUP):
+            fixed, moving = spectra[g]
             fcc, fcs, fsc, fss = fixed[:BLK, :128], fixed[:BLK, 128:], fixed[BLK:, :128], fixed[BLK:, 128:]
             mcc, mcs, msc, mss = moving[:BLK, :128], moving[:BLK, 128:], moving[BLK:, :128], moving[BLK:, 128:]
             ee = fcc * mcc + fss * mss + fcs * mcs + fsc * msc
@@ -352,21 +364,24 @@
             cross = jnp.concatenate(
                 [jnp.concatenate([ee, eo], axis=1), jnp.concatenate([oe, oo], axis=1)], axis=0
             ).astype(jnp.bfloat16)
-            back = dot(inv_left[...], cross).astype(jnp.bfloat16)
-            corr = dot(back, inv_right[...])
-            energy = corr * corr
-            at = h * PATCH_DEV + j % 2 * ROWS + j // 2
-            results.append(
-                (at, jnp.sum(energy, axis=0, keepdims=True), jnp.sum(energy * signed, axis=0, keepdims=True))
-            )
-        for at, plain, by_row in results:
-            sum_e[pl.ds(at, 1), :] = plain
-            sum_r[pl.ds(at, 1), :] = by_row
+            crosses.append(cross)
+        for g in range(GROUP):
+            backs[pl.ds(g * W, W), :] = dot(inv_left[...], crosses[g]).astype(jnp.bfloat16)
+        corr = dot(backs[...], inv_right[...])
+        for g in range(GROUP):
+            h, j, _ = place_of[g]
+            energy = corr[g * W : g * W + W]
+            energy = energy * energy
+            at = pl.ds(h * PATCH_DEV + j % 2 * ROWS + j // 2, 1)
+            sum_e[at, :] = jnp.sum(energy, axis=0, keepdims=True)
+            sum_r[at, :] = jnp.sum(energy * signed, axis=0, keepdims=True)
 
     @pl.when(rounds > 0)
     def _():
         fetch(0, 0)
 
+    for copy in tables:
+        copy.start()
     def one(step, carry):
         slot = step % DEPTH
 
@@ -380,6 +395,8 @@
         work(step, slot)
         return carry
 
+    for copy in tables:
+        copy.wait()
     lax.fori_loop(0, rounds, one, 0)
 
     number = lax.broadcasted_iota(jnp.int32, (NY * PATCH_DEV, 256), 1)
@@ -428,13 +445,11 @@
     own.wait()
 
 
-def settle_kernel(net, mob_band, u_own, flow, out, tgt, mob, ua, ub, vel, mask_up, mask_dn):
+def settle_kernel(net, mob_band, u_own, flow, out, tgt, mob, ua, ub, vel):
     t = lax.axis_index("tile")
     p = lax.axis_index("pair")
-    mask_up[...], mask_dn[...] = row_masks(t)
     lane = lax.broadcasted_iota(jnp.int32, (SPAN, 128), 1)
     node = (lane == 32) | (lane == 96)
-    edge = jnp.zeros((PAD, 128), jnp.float32)
     span = pl.ds(PAD, SPAN)
     vel[...] = jnp.zeros_like(vel)
     ua[...] = jnp.zeros_like(ua)
@@ -443,36 +458,32 @@
         values = net[s]
         for comp in range(2):
             turned = values if comp == 0 else pltpu.roll(values, 127, axis=1)
-            tgt[s, comp, 0, span, :] = jnp.where(node, turned, 0.0)
-        mob[s, span, :] = mob_band[s]
-        mob[s, 0:PAD, :] = edge
-        mob[s, HIGH - PAD :, :] = edge
+            tgt[s, comp, 0, span, :] = (0.3 / 0.35) * jnp.where(node, turned, 0.0)
+        mob[s, 0, span, :] = mob_band[s]
 
     for first in range(0, STEPS, 8):
 
         @pl.loop(0, 4)
         def _(_):
             for u_in, u_out in ((ua, ub), (ub, ua)):
-                for rows in range(PAD + first, HIGH - PAD - first, 8):
-                    relax_block(
-                        tgt, u_in, u_out, vel, lambda s, n, here: mob[s, here, :], mask_up, mask_dn, rows, 1
-                    )
+                relax_step(
+                    t, tgt, u_in, u_out, vel, lambda here: mob[:, :, here, :], PAD + first, HIGH - PAD - first, 1
+                )
 
     middle = pl.ds(PAD + HALO, ROWS)
     lane = lax.broadcasted_iota(jnp.int32, (ROWS, 128), 1)
     row = lax.broadcasted_iota(jnp.int32, (ROWS, 128), 0)
     for comp in range(2):
         moved = jnp.zeros((ROWS, 128), jnp.float32)
-        given = jnp.zeros((ROWS, 128), jnp.float32)
+        given = net[p, HALO : HALO + ROWS, :]
         for s in range(NP):
             moved = jnp.where(p == s, ua[s, comp, 0, middle, :], moved)
-            given = jnp.where(p == s, tgt[s, comp, 0, middle, :], given)
         wide, narrow = pltpu.roll(moved, 96, axis=1), pltpu.roll(moved, 32, axis=1)
         for n, (part, inside) in enumerate(((wide, lane >= 96), (wide, lane < 32), (narrow, lane >= 96), (narrow, lane < 32))):
             columns = pl.ds(128 * n, 128)
             out[comp, :, columns] = u_own[comp, :, columns] + jnp.where(inside, part, 0.0)
-        even = jnp.sum(jnp.where(lane == 32, given, 0.0), axis=1, keepdims=True)
-        odd = jnp.sum(jnp.where(lane == 96, given, 0.0), axis=1, keepdims=True)
+        even = jnp.sum(jnp.where(lane == 32 + comp, given, 0.0), axis=1, keepdims=True)
+        odd = jnp.sum(jnp.where(lane == 96 + comp, given, 0.0), axis=1, keepdims=True)
         spread = jnp.where(lane == 2 * row, even, 0.0) + jnp.where(lane == 2 * row + 1, odd, 0.0)
         flow[comp : comp + 1, :] = jnp.sum(spread, axis=0, keepdims=True)[:, :PATCH_DEV]
 
@@ -490,13 +501,8 @@
     rows_tab = np.zeros((17, FREQ, WIN_ROWS), np.float32)
     for shift in range(17):
         rows_tab[shift, :, shift : shift + W] = left
-    cols_tab = np.zeros((2, MAX_SHIFT + WIN_COLS, 128), np.float32)
-    cols_tab[0, MAX_SHIFT : MAX_SHIFT + W] = right[:, :128]
-    cols_tab[1, MAX_SHIFT : MAX_SHIFT + W] = right[:, 128:]
-    quads_tab = np.zeros((4, 256, 256), np.float32)
-    for q in range(4):
-        quads_tab[q, :128] = right[:128]
-        quads_tab[q, 128 + 32 * q : 160 + 32 * q] = right[128:]
+    cols_tab = np.zeros((256, 256), np.float32)
+    cols_tab[:W] = right
     weight = np.full((HALF, 1), 2.0, np.float32)
     weight[0] = weight[-1] = 1.0
     inv_left = np.zeros((W, FREQ), np.float32)
@@ -504,7 +510,7 @@
     inv_right = np.zeros((256, 256), np.float32)
     inv_right[:HALF, :W], inv_right[128 : 128 + HALF, :W] = weight * cos[:HALF], -2.0 * sin[:HALF]
     half = lambda table: table.astype(ml_dtypes.bfloat16)
-    return half(rows_tab), cols_tab, half(quads_tab), half(inv_left), half(inv_right)
+    return half(rows_tab), half(cols_tab), half(inv_left), half(inv_right)
 
 
 def any_spec():
@@ -513,6 +519,35 @@
 
 def vmem_spec():
     return pl.BlockSpec(memory_space=pltpu.VMEM)
+
+
+def flow_call(gmeta, gi, gpl, gpr):
+    f32, bf16 = jnp.float32, jnp.bfloat16
+    tables = [jnp.asarray(table) for table in make_tables()]
+    return pl.pallas_call(
+        flow_kernel,
+        out_shape=jax.ShapeDtypeStruct((NY, ROWS, 128), f32),
+        in_specs=[pl.BlockSpec(memory_space=pltpu.SMEM)] + [any_spec()] * 7,
+        out_specs=vmem_spec(),
+        scratch_shapes=[
+            pltpu.SMEM((NY * PATCH_DEV + 1,), jnp.int32),
+            pltpu.VMEM((17, FREQ, WIN_ROWS), bf16),
+            pltpu.VMEM((256, 256), bf16),
+            pltpu.VMEM((W, FREQ), bf16),
+            pltpu.VMEM((256, 256), bf16),
+            pltpu.VMEM((DEPTH, GROUP, WIN_ROWS, WIN_COLS), bf16),
+            pltpu.VMEM((DEPTH, GROUP, W, 256), bf16),
+            pltpu.VMEM((GROUP * (WIN_ROWS + W), 256), bf16),
+            pltpu.VMEM((GROUP * (WIN_ROWS + W), 256), bf16),
+            pltpu.VMEM((GROUP * W, 256), bf16),
+            pltpu.VMEM((NY * PATCH_DEV, 256), f32),
+            pltpu.VMEM((NY * PATCH_DEV, 256), f32),
+            pltpu.SemaphoreType.DMA((DEPTH, GROUP, 4)),
+            pltpu.SemaphoreType.DMA((4,)),
+        ],
+        compiler_params=pltpu.CompilerParams(vmem_limit_bytes=32 * 2**20),
+        name="patch_flows",
+    )(gmeta, gi, gpl, gpr, *tables)
 
 
 def shards(fixed_image, moving_patches, owners, offsets, mobility, prior_flow):
@@ -535,12 +570,12 @@
         scratch_shapes=[
             pltpu.VMEM((PATCH_DEV, W, W), bf16),
             pltpu.VMEM((PATCH_DEV // 4, W, 128), bf16),
-            pltpu.VMEM((3, TILES_X, ROWS, 128), f32),
+            pltpu.VMEM((3, TILES_X, ROWS, 128), bf16),
+            pltpu.VMEM((NP, 3, TILES_X, SPAN, 128), bf16),
             pltpu.VMEM((NP, 3, TILES_X, HIGH, 128), f32),
-            pltpu.VMEM((2, NP, 2, TILES_X, HIGH, 128), f32),
             pltpu.VMEM((NP, 2, TILES_X, HIGH, 128), f32),
-            pltpu.VMEM((HIGH, 128), f32),
-            pltpu.VMEM((HIGH, 128), f32),
+            pltpu.VMEM((NP, 2, TILES_X, HIGH, 128), f32),
+            pltpu.VMEM((NP, 2, TILES_X, HIGH, 128), f32),
             dma((5,)), dma((2, 6)), dma((2, 6)), dma((2, 8)), dma((2, 8)), dma((16,)), dma((16,)),
             dma((3,)), dma((3,)), dma((19,)), dma((19,)),
         ],
@@ -549,23 +584,7 @@
         ),
         name="gather_and_relax",
     )(fixed_image[0], moving_patches[0], meta, prior_flow[0], mobility[0])
-    tables = [jnp.asarray(table) for table in make_tables()]
-    ep = pl.pallas_call(
-        flow_kernel,
-        out_shape=sds((NY, ROWS, 128), f32),
-        in_specs=[pl.BlockSpec(memory_space=pltpu.SMEM)] + [any_spec()] * 3 + [vmem_spec()] * 5,
-        out_specs=vmem_spec(),
-        scratch_shapes=[
-            pltpu.SMEM((NY * PATCH_DEV + 1,), jnp.int32),
-            pltpu.VMEM((DEPTH, GROUP, WIN_ROWS, WIN_COLS), bf16),
-            pltpu.VMEM((DEPTH, GROUP, W, 256), bf16),
-            pltpu.VMEM((NY * PATCH_DEV, 256), f32),
-            pltpu.VMEM((NY * PATCH_DEV, 256), f32),
-            dma((DEPTH, GROUP, 3)),
-        ],
-        compiler_params=pltpu.CompilerParams(vmem_limit_bytes=32 * 2**20),
-        name="patch_flows",
-    )(gmeta, gi, gpl, gpr, *tables)
+    ep = flow_call(gmeta, gi, gpl, gpr)
     net = pl.pallas_call(
         share_kernel,
         out_shape=sds((NP, SPAN, 128), f32),
@@ -585,12 +604,10 @@
         out_specs=(vmem_spec(), vmem_spec()),
         scratch_shapes=[
             pltpu.VMEM((NP, 2, 1, HIGH, 128), f32),
-            pltpu.VMEM((NP, HIGH, 128), f32),
+            pltpu.VMEM((NP, 1, HIGH, 128), f32),
             pltpu.VMEM((NP, 2, 1, HIGH, 128), f32),
             pltpu.VMEM((NP, 2, 1, HIGH, 128), f32),
             pltpu.VMEM((NP, 2, 1, HIGH, 128), f32),
-            pltpu.VMEM((HIGH, 128), f32),
-            pltpu.VMEM((HIGH, 128), f32),
         ],
         compiler_params=pltpu.CompilerParams(vmem_limit_bytes=32 * 2**20),
         name="settle",

time: 303 us -> 120 us (0.40)
  Pallas kernels: 295 us -> 113 us
    pallas_call x1, Pallas kernels: 236 us -> 77.5 us  [shards(): pl.pallas_call(gather_kernel, out_shape=(sds((NZ * NC, TILE, TILE), bf16)...]
    pallas_call x1, Pallas kernels: 29.5 us -> 11.2 us  [flow_call(): pl.pallas_call(flow_kernel, out_shape=jax.ShapeDtypeStruct((NY, ROWS, 128...]
    pallas_call x1, Pallas kernels: 10.2 us -> 6.4 us  [shards(): pl.pallas_call(settle_kernel, out_shape=(sds((2, PATCH_DEV), f32), sds((2...]
where the time goes in v2:
time: 120 us
  Pallas kernels  113 us (94%)
  local copies, waits for them, and re-layouts  5.91 us (5%)
    pallas_call x1, Pallas kernels, shards(): pl.pallas_call(gather_kernel, out_shape=(sds((NZ * NC, TILE, TILE), bf16)...  77.5 us
    pallas_call x1, Pallas kernels, shards(): pl.pallas_call(share_kernel, out_shape=sds((NP, SPAN, 128), f32), in_spec...  17.5 us
    pallas_call x1, Pallas kernels, flow_call(): pl.pallas_call(flow_kernel, out_shape=jax.ShapeDtypeStruct((NY, ROWS, 128...  11.2 us
    pallas_call x1, Pallas kernels, shards(): pl.pallas_call(settle_kernel, out_shape=(sds((2, PATCH_DEV), f32), sds((2...  6.4 us
    unnamed x20, local copies, waits for them, and re-layouts  5.91 us

profile of v2, /device:TPU:1, one launch (start us, length us, event | category | flops | bytes accessed | tf_op | source)
XLA Modules:
  0.0 119.9 jit_solution(6212439725252508472)
XLA Ops:
  0.6 0.7 pad_add_fusion
  1.3 0.0 copy-start
  1.3 1.7 %copy-done = bf16[1,32,160,160]{3,2,1,0:T(8,128)(2,1)S(1)} copy-done((bf16[1,32,160,160]{3,2,1,0:T(8,128)(2,1)S(1)}, bf16[1,32,160,160]{3,2,1,0:T(8,128)(2,1)}, u32[]{:S(2)}) %copy-start) | copy-done | bytes 1638424
  3.1 0.0 copy-start.3
  3.1 1.0 copy-done.3
  4.1 0.0 copy-start.8
  4.1 0.8 copy-done.8
  5.0 0.0 copy-start.9
  5.0 0.8 copy-done.9
  5.7 0.0 copy-start.1
  5.7 0.0 copy-start.4
  5.7 0.0 copy-start.5
  5.7 77.5 %gather_and_relax.1 = (bf16[16,512,512]{2,1,0:T(8,128)(2,1)S(1)}, bf16[4,32,160,128]{3,2,1,0:T(8,128)(2,1)S(1)}, bf16[4,8,160,128]{3,2,1,0:T(8,128)(2,1)S(1)}, s...) custom-call(bf16[512,512]{1,0:T(8,128)(2,1)S(1)} %bitcast.10, ...), custom_call_target="tpu_custom_call" | custom-call | tf_op jit(solution)/shard_map/gather_and_relax/pallas_call | solution.py:558
  83.2 0.0 copy-done.1
  83.2 0.0 copy-done.4
  83.2 0.0 copy-done.5
  83.2 0.0 copy-done.7
  83.2 11.2 %patch_flows.1.ep = f32[4,16,128]{2,1,0:T(8,128)S(1)} custom-call(s32[4,8,128]{2,1,0:T(8,128)S(1)} %get-tuple-element.10.meta, bf16[16,512,512]{2,1,0:T(8,128)(2,1)S(1)} %get-tuple-element.11.gi, bf16[4,32,160,128]{3,2,1,0:T(8,128)(2,1)S(1)} %get-tuple-element.12.gpl, bf16[4,8,160,128]{3,2,1,0:T(8,128)(2,1)S(1)} %get-tuple-element.13.gpr, ...), custom_call_target="tpu_custom_call" | custom-call | tf_op jit(solution)/shard_map/patch_flows/pallas_call | solution.py:527
  94.5 0.0 copy-start.6
  94.5 0.6 copy-done.6
  95.1 17.5 %share_flows.1.net = f32[4,80,128]{2,1,0:T(8,128)} custom-call(f32[4,16,128]{2,1,0:T(8,128)} %copy-done.6), custom_call_target="tpu_custom_call" | custom-call | tf_op jit(solution)/shard_map/share_flows/pallas_call | solution.py:588
  112.6 0.0 copy-start.2
  112.6 0.9 copy-done.2
  113.5 6.4 %settle.1 = (f32[2,32]{1,0:T(2,128)}, f32[2,16,512]{2,1,0:T(8,128)}) custom-call(f32[4,80,128]{2,1,0:T(8,128)S(1)} %copy-done.2, f32[4,80,128]{2,1,0:T(8,128)S(1)} %get-tuple-element.14.mob_band, f32[2,16,512]{2,1,0:T(8,128)S(1)} %get-tuple-element.15.u_own), custom_call_target="tpu_custom_call" | custom-call | tf_op jit(solution)/shard_map/settle/pallas_call | solution.py:600
  (2 shorter events, 0.0 us)
Async XLA Ops:
  1.3 1.7 %copy-start = (bf16[1,32,160,160]{3,2,1,0:T(8,128)(2,1)S(1)}, bf16[1,32,160,160]{3,2,1,0:T(8,128)(2,1)}, u32[]{:S(2)}) copy-start(bf16[1,32,160,160]{3,2,1,0:T(8,128)(2,1)} %param.11) | copy-start | bytes 4915204
  3.1 1.0 copy-start.3
  4.1 0.8 copy-start.8
  5.0 0.8 copy-start.9
  5.7 77.5 %copy-start.1 = (bf16[17,176,176]{2,1,0:T(8,128)(2,1)S(1)}, bf16[17,176,176]{2,1,0:T(8,128)(2,1)}, u32[]{:S(2)}) copy-start(bf16[17,176,176]{2,1,0:T(8,128)(2,1)} %constant.10.clone.rows_hbm) | copy-start | bytes 3159556
  5.7 77.5 %copy-start.4 = (bf16[256,256]{1,0:T(8,128)(2,1)S(1)}, bf16[256,256]{1,0:T(8,128)(2,1)}, u32[]{:S(2)}) copy-start(bf16[256,256]{1,0:T(8,128)(2,1)} %constant.13.clone.right_hbm) | copy-start | bytes 393220
  5.7 77.5 %copy-start.5 = (bf16[256,256]{1,0:T(8,128)(2,1)S(1)}, bf16[256,256]{1,0:T(8,128)(2,1)}, u32[]{:S(2)}) copy-start(bf16[256,256]{1,0:T(8,128)(2,1)} %constant.11.clone.cols_hbm) | copy-start | bytes 393220
  5.7 77.5 %copy-start.7 = (bf16[160,176]{1,0:T(8,128)(2,1)S(1)}, bf16[160,176]{1,0:T(8,128)(2,1)}, u32[]{:S(2)}) copy-start(bf16[160,176]{1,0:T(8,128)(2,1)} %constant.12.clone.left_hbm) | copy-start | bytes 168964
  94.5 0.6 copy-start.6
  112.6 0.9 copy-start.2

commit v3 on v2

--- a/solution.py
+++ b/solution.py
@@ -71,7 +71,7 @@
     own = PAD + HALO
     for rows in range(first, last, 8):
         here = pl.ds(rows, 8)
-        for comp in range(2):
+        for comp in range(u_in.shape[1]):
             u = u_in[:, comp, :, here, :]
             above = u_in[:, comp, :, pl.ds(rows - 1, 8), :]
             below = u_in[:, comp, :, pl.ds(rows + 1, 8), :]
@@ -92,9 +92,9 @@
 
 
 def gather_kernel(
-    img, pat, meta, prior, mob, gi, gpl, gpr, gmeta, u_own, mob_band,
-    pv, pr, own, net, target, ua, ub, vel,
-    lsem, ysend, yrecv, zsend, zrecv, dsend, drecv, msend, mrecv, hsend, hrecv,
+    img, pat, meta, prior_hbm, mob_hbm, gi, gpl, gpr, gmeta, u_own, mob_band,
+    prior, mob, pv, pr, fine, own, net, target, mobs, ua, ub, vel, res, got,
+    lsem, ysend, yrecv, zsend, zrecv, dsend, drecv, msend, mrecv, hsend, hrecv, rsend, rrecv,
 ):
     t, y, z, c = my_place()
     p = lax.axis_index("pair")
@@ -104,6 +104,12 @@
     sibling = device_at(y, z, 1 - c)
     stage = pltpu.make_async_copy(pat, pv, lsem.at[0])
     stage.start()
+    strips = [
+        pltpu.make_async_copy(prior_hbm, prior, lsem.at[2]),
+        pltpu.make_async_copy(mob_hbm, mob, lsem.at[3]),
+    ]
+    for copy in strips:
+        copy.start()
     mine = z * NC + c
     keep = pltpu.make_async_copy(img, gi.at[mine], lsem.at[1])
     keep.start()
@@ -130,16 +136,6 @@
 
     start(y_left(hi, y, 0, right_y, 0), yr)
     start(y_left(lo, y, 1, left_y, 0), yl)
-
-    for n in range(TILES_X):
-        columns = pl.ds(128 * n, 128)
-        own[0:2, n] = prior[:, :, columns].astype(jnp.bfloat16)
-        own[2, n] = mob[:, columns].astype(jnp.bfloat16)
-    meshes = []
-    for n, (dp, d, device) in enumerate(halo):
-        rows = pl.ds(ROWS * (2 - d), ROWS)
-        copy = remote(own, net.at[p, :, :, rows, :], hsend.at[n], hrecv.at[n], device)
-        start(copy, meshes)
 
     half = TILE // 2
     zr, zl, dd = [], [], []
@@ -148,6 +144,21 @@
         start(remote(img.at[rs], gi.at[mine, rs], zsend.at[0, q], zrecv.at[0, q], right_z), zr)
         rs = pl.ds((1 - q) * half, half)
         start(remote(img.at[rs], gi.at[mine, rs], zsend.at[1, q], zrecv.at[1, q], left_z), zl)
+    for copy in strips:
+        copy.wait()
+    for n in range(TILES_X):
+        columns = pl.ds(128 * n, 128)
+        fine[0:2, n] = prior[:, :, columns]
+        fine[2, n] = mob[:, columns]
+    for v in range(NP):
+        own[v, 0:3] = fine[v % 2, v // 2 : v // 2 + 3].astype(jnp.bfloat16)
+        own[v, 3:7] = fine[2].astype(jnp.bfloat16)
+    meshes = []
+    for n, (dp, d, device) in enumerate(halo):
+        rows = pl.ds(ROWS * (2 - d), ROWS)
+        copy = remote(own.at[(p + dp) % NP], net.at[p, :, rows, :], hsend.at[n], hrecv.at[n], device)
+        start(copy, meshes)
+
     start(y_left(lo, y, 0, right_y, 1), yr)
     start(y_left(hi, y, 1, left_y, 1), yl)
     metas = []
@@ -185,12 +196,13 @@
             start(remote(block, block, dsend.at[n], drecv.at[n], sibling), dd)
 
     middle = pl.ds(PAD + HALO, ROWS)
+    comp, side = p % 2, p // 2
 
     def begin():
         for copy in meshes:
             copy.wait_recv()
-        net[p, :, :, HALO : HALO + ROWS, :] = own[...]
-        edge = jnp.zeros((NP, 2, TILES_X, PAD, 128), jnp.float32)
+        net[p, :, HALO : HALO + ROWS, :] = own[p]
+        edge = jnp.zeros((NP, 1, 3, PAD, 128), jnp.float32)
         for ref in (ua, ub):
             ref[:, :, :, 0:PAD, :] = edge
             ref[:, :, :, HIGH - PAD :, :] = edge
@@ -199,61 +211,66 @@
         def _(s):
             for b in range(SPAN // ROWS):
                 rows = pl.ds(PAD + ROWS * b, ROWS)
-                values = net[s, :, :, ROWS * b : ROWS * b + ROWS, :].astype(jnp.float32)
-                ua[s, :, :, rows, :] = values[0:2]
-                ub[s, :, :, rows, :] = values[0:2]
-                vel[s, :, :, rows, :] = jnp.zeros_like(values[0:2])
-                target[s, 0:2, :, rows, :] = (0.3 / 0.35) * values[0:2]
-                target[s, 2, :, rows, :] = 0.35 * values[2]
-
-        for n in range(TILES_X):
-            columns = pl.ds(128 * n, 128)
-            values = prior[:, :, columns]
-            ua[p, :, n, middle, :] = values
-            target[p, 0:2, n, middle, :] = (0.3 / 0.35) * values
-            target[p, 2, n, middle, :] = 0.35 * mob[:, columns]
+                values = net[s, :, ROWS * b : ROWS * b + ROWS, :].astype(jnp.float32)
+                ua[s, 0, :, rows, :] = values[0:3]
+                ub[s, 0, :, rows, :] = values[0:3]
+                vel[s, 0, :, rows, :] = jnp.zeros_like(values[0:3])
+                target[s, 0, :, rows, :] = (0.3 / 0.35) * values[0:3]
+                mobs[s, :, rows, :] = 0.35 * values[3:7]
+
+        values = fine[comp, pl.ds(side, 3)]
+        ua[p, 0, :, middle, :] = values
+        target[p, 0, :, middle, :] = (0.3 / 0.35) * values
+        mobs[p, :, middle, :] = 0.35 * fine[2]
 
     def relax(first):
         @pl.loop(0, 4)
         def _(_):
             for u_in, u_out in ((ua, ub), (ub, ua)):
                 relax_step(
-                    t, target, u_in, u_out, vel, lambda here: target[:, 2, :, here, :],
-                    PAD + first, HIGH - PAD - first, TILES_X,
+                    t, target, u_in, u_out, vel, lambda here: mobs[:, pl.ds(side, 3), here, :],
+                    PAD + first, HIGH - PAD - first, 3,
                 )
 
+    def forward_y():
+        for copy in (yr[0], yl[0], pairs[0], pairs[1]):
+            copy.wait_recv()
+        before, after = (y + NY - 1) % NY, (y + 1) % NY
+        for side, first, which, groups, device in ((0, before, hi, ghi, right_y), (1, after, lo, glo, left_y)):
+            block = gpl.at[first, which]
+            start(remote(block, block, ysend.at[side, 2], yrecv.at[side, 2], device), far)
+            block = gpr.at[first, groups]
+            start(remote(block, block, ysend.at[side, 5], yrecv.at[side, 5], device), far)
+
+    far = []
     forward_z(1, 0)
     forward_z(1, 1)
+    forward_z(2, 0)
+    forward_y()
     begin()
     relax(0)
-    forward_z(2, 0)
-    yr[0].wait_recv()
-    yl[0].wait_recv()
-    pairs[0].wait_recv()
-    pairs[1].wait_recv()
-    before, after = (y + NY - 1) % NY, (y + 1) % NY
-    far = []
-    for side, first, which, groups, device in ((0, before, hi, ghi, right_y), (1, after, lo, glo, left_y)):
-        block = gpl.at[first, which]
-        start(remote(block, block, ysend.at[side, 2], yrecv.at[side, 2], device), far)
-        block = gpr.at[first, groups]
-        start(remote(block, block, ysend.at[side, 5], yrecv.at[side, 5], device), far)
+    forward_z(2, 1)
     relax(8)
-    forward_z(2, 1)
+    forward_z(3, 0)
     relax(16)
-    forward_z(3, 0)
+    forward_z(3, 1)
     relax(24)
-    forward_z(3, 1)
+    res[...] = ua[:, 0, pl.ds(side, 2), middle, :]
+    results = []
+    for d in range(1, NP):
+        to = (p + d) % NP
+        start(remote(res.at[to], got.at[p], rsend.at[d - 1], rrecv.at[d - 1], {"pair": to}), results)
+    got[p] = res[p]
     forward_z(4, 0)
-
-    for n in range(TILES_X):
-        moved = jnp.zeros((2, ROWS, 128), jnp.float32)
-        for s in range(NP):
-            moved = jnp.where(p == s, ua[s, :, n, middle, :], moved)
-        u_own[:, :, 128 * n : 128 * n + 128] = moved
+    for copy in results:
+        copy.wait_recv()
+    for v in range(NP):
+        for n in range(2):
+            first = 128 * (v // 2 * 2 + n)
+            u_own[v % 2, :, first : first + 128] = got[v, n]
     lane = lax.broadcasted_iota(jnp.int32, (SPAN, 128), 1)
     for s in range(NP):
-        parts = [target[s, 2, n, PAD : PAD + SPAN, :] for n in range(4)]
+        parts = [mobs[s, n, PAD : PAD + SPAN, :] for n in range(4)]
         low = jnp.where(lane < 32, pltpu.roll(parts[0], 32, axis=1), pltpu.roll(parts[1], 32, axis=1))
         top = jnp.where(lane < 96, pltpu.roll(parts[2], 96, axis=1), pltpu.roll(parts[3], 96, axis=1))
         mob_band[s] = jnp.where(lane < 64, low, top)
@@ -278,6 +295,9 @@
             ((cols_hbm, cols_tab), (rows_hbm, rows_tab), (left_hbm, inv_left), (right_hbm, inv_right))
         )
     ]
+
+    for copy in tables:
+        copy.start()
 
     def note(h, count):
         for j in range(PATCH_DEV):
@@ -380,8 +400,6 @@
     def _():
         fetch(0, 0)
 
-    for copy in tables:
-        copy.start()
     def one(step, carry):
         slot = step % DEPTH
 
@@ -517,6 +535,10 @@
     return pl.BlockSpec(memory_space=pl.ANY)
 
 
+def hbm_spec():
+    return pl.BlockSpec(memory_space=pltpu.HBM)
+
+
 def vmem_spec():
     return pl.BlockSpec(memory_space=pltpu.VMEM)
 
@@ -527,7 +549,7 @@
     return pl.pallas_call(
         flow_kernel,
         out_shape=jax.ShapeDtypeStruct((NY, ROWS, 128), f32),
-        in_specs=[pl.BlockSpec(memory_space=pltpu.SMEM)] + [any_spec()] * 7,
+        in_specs=[pl.BlockSpec(memory_space=pltpu.SMEM)] + [any_spec()] * 3 + [hbm_spec()] * 4,
         out_specs=vmem_spec(),
         scratch_shapes=[
             pltpu.SMEM((NY * PATCH_DEV + 1,), jnp.int32),
@@ -545,7 +567,7 @@
             pltpu.SemaphoreType.DMA((DEPTH, GROUP, 4)),
             pltpu.SemaphoreType.DMA((4,)),
         ],
-        compiler_params=pltpu.CompilerParams(vmem_limit_bytes=32 * 2**20),
+        compiler_params=pltpu.CompilerParams(vmem_limit_bytes=60 * 2**20),
         name="patch_flows",
     )(gmeta, gi, gpl, gpr, *tables)
 
@@ -565,22 +587,28 @@
             sds((2, ROWS, COLS), f32),
             sds((NP, SPAN, 128), f32),
         ),
-        in_specs=[any_spec(), any_spec(), vmem_spec(), vmem_spec(), vmem_spec()],
+        in_specs=[hbm_spec(), hbm_spec(), vmem_spec(), hbm_spec(), hbm_spec()],
         out_specs=(any_spec(), any_spec(), any_spec(), any_spec(), vmem_spec(), vmem_spec()),
         scratch_shapes=[
+            pltpu.VMEM((2, ROWS, COLS), f32),
+            pltpu.VMEM((ROWS, COLS), f32),
             pltpu.VMEM((PATCH_DEV, W, W), bf16),
             pltpu.VMEM((PATCH_DEV // 4, W, 128), bf16),
-            pltpu.VMEM((3, TILES_X, ROWS, 128), bf16),
-            pltpu.VMEM((NP, 3, TILES_X, SPAN, 128), bf16),
-            pltpu.VMEM((NP, 3, TILES_X, HIGH, 128), f32),
-            pltpu.VMEM((NP, 2, TILES_X, HIGH, 128), f32),
-            pltpu.VMEM((NP, 2, TILES_X, HIGH, 128), f32),
-            pltpu.VMEM((NP, 2, TILES_X, HIGH, 128), f32),
+            pltpu.VMEM((3, TILES_X, ROWS, 128), f32),
+            pltpu.VMEM((NP, 7, ROWS, 128), bf16),
+            pltpu.VMEM((NP, 7, SPAN, 128), bf16),
+            pltpu.VMEM((NP, 1, 3, HIGH, 128), f32),
+            pltpu.VMEM((NP, TILES_X, HIGH, 128), f32),
+            pltpu.VMEM((NP, 1, 3, HIGH, 128), f32),
+            pltpu.VMEM((NP, 1, 3, HIGH, 128), f32),
+            pltpu.VMEM((NP, 1, 3, HIGH, 128), f32),
+            pltpu.VMEM((NP, 2, ROWS, 128), f32),
+            pltpu.VMEM((NP, 2, ROWS, 128), f32),
             dma((5,)), dma((2, 6)), dma((2, 6)), dma((2, 8)), dma((2, 8)), dma((16,)), dma((16,)),
-            dma((3,)), dma((3,)), dma((19,)), dma((19,)),
+            dma((3,)), dma((3,)), dma((19,)), dma((19,)), dma((3,)), dma((3,)),
         ],
         compiler_params=pltpu.CompilerParams(
-            collective_id=0, has_side_effects=True, vmem_limit_bytes=32 * 2**20
+            collective_id=0, has_side_effects=True, vmem_limit_bytes=60 * 2**20
         ),
         name="gather_and_relax",
     )(fixed_image[0], moving_patches[0], meta, prior_flow[0], mobility[0])
@@ -609,7 +637,7 @@
             pltpu.VMEM((NP, 2, 1, HIGH, 128), f32),
             pltpu.VMEM((NP, 2, 1, HIGH, 128), f32),
         ],
-        compiler_params=pltpu.CompilerParams(vmem_limit_bytes=32 * 2**20),
+        compiler_params=pltpu.CompilerParams(vmem_limit_bytes=60 * 2**20),
         name="settle",
     )(net, mob_band, u_own)
     return flow[None], out[None]

time: 120 us -> 111 us (0.925)
  local copies, waits for them, and re-layouts: 5.91 us -> 0.6 us
  Pallas kernels: 113 us -> 109 us
    unnamed x20 -> x0, local copies, waits for them, and re-layouts: 5.91 us -> none
    pallas_call x1, Pallas kernels: 77.5 us -> 71.6 us  [shards(): pl.pallas_call(gather_kernel, out_shape=(sds((NZ * NC, TILE, TILE), bf16)...]
    pallas_call x1, Pallas kernels: 11.2 us -> 15.9 us  [flow_call(): pl.pallas_call(flow_kernel, out_shape=jax.ShapeDtypeStruct((NY, ROWS, 128...]
    pallas_call x1, Pallas kernels: 17.5 us -> 13.8 us  [shards(): pl.pallas_call(share_kernel, out_shape=sds((NP, SPAN, 128), f32), in_spec...]
where the time goes in v3:
time: 111 us
  Pallas kernels  109 us (98%)
    pallas_call x1, Pallas kernels, shards(): pl.pallas_call(gather_kernel, out_shape=(sds((NZ * NC, TILE, TILE), bf16)...  71.6 us
    pallas_call x1, Pallas kernels, flow_call(): pl.pallas_call(flow_kernel, out_shape=jax.ShapeDtypeStruct((NY, ROWS, 128...  15.9 us
    pallas_call x1, Pallas kernels, shards(): pl.pallas_call(share_kernel, out_shape=sds((NP, SPAN, 128), f32), in_spec...  13.8 us
    pallas_call x1, Pallas kernels, shards(): pl.pallas_call(settle_kernel, out_shape=(sds((2, PATCH_DEV), f32), sds((2...  7.45 us

profile of v3, /device:TPU:1, one launch (start us, length us, event | category | flops | bytes accessed | tf_op | source)
XLA Modules:
  0.0 110.6 jit_solution(14875319249259692975)
XLA Ops:
  0.6 0.7 pad_add_fusion
  1.3 0.6 pad.4.meta
  1.9 71.6 %gather_and_relax.1 = (bf16[16,512,512]{2,1,0:T(8,128)(2,1)}, bf16[4,32,160,128]{3,2,1,0:T(8,128)(2,1)}, bf16[4,8,160,128]{3,2,1,0:T(8,128)(2,1)}, s32[4,8,128]{...) custom-call(bf16[512,512]{1,0:T(8,128)(2,1)} %bitcast.10, bf16[32,160,160]{2,1,0:T(8,128)(2,1)} %bitcast.9, ...), custom_call_target="tpu_custom_call" | custom-call | tf_op jit(solution)/shard_map/gather_and_relax/pallas_call | solution.py:580
  73.5 15.9 %patch_flows.1.ep = f32[4,16,128]{2,1,0:T(8,128)} custom-call(s32[4,8,128]{2,1,0:T(8,128)} %get-tuple-element.10.meta, bf16[16,512,512]{2,1,0:T(8,128)(2,1)} %get-tuple-element.11.gi, bf16[4,32,160,128]{3,2,1,0:T(8,128)(2,1)} %get-tuple-element.12.gpl, bf16[4,8,160,128]{3,2,1,0:T(8,128)(2,1)} %get-tuple-element.13.gpr, ...), custom_call_target="tpu_custom_call" | custom-call | tf_op jit(solution)/shard_map/patch_flows/pallas_call | solution.py:549
  89.4 13.8 %share_flows.1.net = f32[4,80,128]{2,1,0:T(8,128)} custom-call(f32[4,16,128]{2,1,0:T(8,128)} %patch_flows.1.ep), custom_call_target="tpu_custom_call" | custom-call | tf_op jit(solution)/shard_map/share_flows/pallas_call | solution.py:616
  103.2 7.5 %settle.1 = (f32[2,32]{1,0:T(2,128)}, f32[2,16,512]{2,1,0:T(8,128)}) custom-call(f32[4,80,128]{2,1,0:T(8,128)} %share_flows.1.net, f32[4,80,128]{2,1,0:T(8,128)} %get-tuple-element.14.mob_band, f32[2,16,512]{2,1,0:T(8,128)} %get-tuple-element.15.u_own), custom_call_target="tpu_custom_call" | custom-call | tf_op jit(solution)/shard_map/settle/pallas_call | solution.py:628

commit v4 on v3

--- a/solution.py
+++ b/solution.py
@@ -92,8 +92,8 @@
 
 
 def gather_kernel(
-    img, pat, meta, prior_hbm, mob_hbm, gi, gpl, gpr, gmeta, u_own, mob_band,
-    prior, mob, pv, pr, fine, own, net, target, mobs, ua, ub, vel, res, got,
+    img, pat, owners, offsets, prior_hbm, mob_hbm, gi, gpl, gpr, gmeta, u_own, mob_band,
+    meta, own_v, off_v, prior, mob, pv, pr, fine, own, net, target, mobs, ua, ub, vel, res, got,
     lsem, ysend, yrecv, zsend, zrecv, dsend, drecv, msend, mrecv, hsend, hrecv, rsend, rrecv,
 ):
     t, y, z, c = my_place()
@@ -107,6 +107,8 @@
     strips = [
         pltpu.make_async_copy(prior_hbm, prior, lsem.at[2]),
         pltpu.make_async_copy(mob_hbm, mob, lsem.at[3]),
+        pltpu.make_async_copy(owners, own_v, lsem.at[4]),
+        pltpu.make_async_copy(offsets, off_v, lsem.at[5]),
     ]
     for copy in strips:
         copy.start()
@@ -146,6 +148,8 @@
         start(remote(img.at[rs], gi.at[mine, rs], zsend.at[1, q], zrecv.at[1, q], left_z), zl)
     for copy in strips:
         copy.wait()
+    meta[0:1, 0:PATCH_DEV] = own_v[...]
+    meta[1:3, 0:PATCH_DEV] = off_v[...]
     for n in range(TILES_X):
         columns = pl.ds(128 * n, 128)
         fine[0:2, n] = prior[:, :, columns]
@@ -435,9 +439,18 @@
         out[h] = block
 
 
-def share_kernel(ep, net, got, total, fsend, frecv, hsend, hrecv, lsem):
+def settle_kernel(
+    ep, mob_hbm, own_hbm, flow, out,
+    got, total, net, mob_band, u_own, tgt, mob, ua, ub, vel, fsend, frecv, hsend, hrecv, lsem,
+):
     t, y, z, c = my_place()
     p = lax.axis_index("pair")
+    local = [
+        pltpu.make_async_copy(mob_hbm, mob_band, lsem.at[0]),
+        pltpu.make_async_copy(own_hbm, u_own, lsem.at[1]),
+    ]
+    for copy in local:
+        copy.start()
     homes = [device_at((y + d) % NY, z, c) for d in range(1, NY)]
     halo = list(halo_targets(t, p))
     greet(homes + [device for _, _, device in halo])
@@ -446,6 +459,13 @@
         copy = remote(ep.at[(y + n + 1) % NY], got.at[n], fsend.at[n], frecv.at[n], device)
         copy.start()
         first.append(copy)
+    span = pl.ds(PAD, SPAN)
+    vel[...] = jnp.zeros_like(vel)
+    ua[...] = jnp.zeros_like(ua)
+    ub[...] = jnp.zeros_like(ub)
+    for copy in local:
+        copy.wait()
+    mob[:, 0, span, :] = mob_band[...]
     for copy in first:
         copy.wait_recv()
     total[...] = ep[y] + got[0] + got[1] + got[2]
@@ -454,38 +474,25 @@
         copy = remote(total, net.at[p, pl.ds(ROWS * (2 - d), ROWS), :], hsend.at[n], hrecv.at[n], device)
         copy.start()
         second.append(copy)
-    own = pltpu.make_async_copy(total, net.at[p, pl.ds(HALO, ROWS), :], lsem)
-    own.start()
+    net[p, HALO : HALO + ROWS, :] = total[...]
     for copy in second:
         copy.wait_recv()
-    for copy in first + second:
-        copy.wait_send()
-    own.wait()
-
-
-def settle_kernel(net, mob_band, u_own, flow, out, tgt, mob, ua, ub, vel):
-    t = lax.axis_index("tile")
-    p = lax.axis_index("pair")
+
     lane = lax.broadcasted_iota(jnp.int32, (SPAN, 128), 1)
     node = (lane == 32) | (lane == 96)
-    span = pl.ds(PAD, SPAN)
-    vel[...] = jnp.zeros_like(vel)
-    ua[...] = jnp.zeros_like(ua)
-    ub[...] = jnp.zeros_like(ub)
     for s in range(NP):
         values = net[s]
         for comp in range(2):
             turned = values if comp == 0 else pltpu.roll(values, 127, axis=1)
             tgt[s, comp, 0, span, :] = (0.3 / 0.35) * jnp.where(node, turned, 0.0)
-        mob[s, 0, span, :] = mob_band[s]
-
-    for first in range(0, STEPS, 8):
+
+    for start in range(0, STEPS, 8):
 
         @pl.loop(0, 4)
         def _(_):
             for u_in, u_out in ((ua, ub), (ub, ua)):
                 relax_step(
-                    t, tgt, u_in, u_out, vel, lambda here: mob[:, :, here, :], PAD + first, HIGH - PAD - first, 1
+                    t, tgt, u_in, u_out, vel, lambda here: mob[:, :, here, :], PAD + start, HIGH - PAD - start, 1
                 )
 
     middle = pl.ds(PAD + HALO, ROWS)
@@ -504,6 +511,8 @@
         odd = jnp.sum(jnp.where(lane == 96 + comp, given, 0.0), axis=1, keepdims=True)
         spread = jnp.where(lane == 2 * row, even, 0.0) + jnp.where(lane == 2 * row + 1, odd, 0.0)
         flow[comp : comp + 1, :] = jnp.sum(spread, axis=0, keepdims=True)[:, :PATCH_DEV]
+    for copy in first + second:
+        copy.wait_send()
 
 
 def make_tables():
@@ -573,7 +582,6 @@
 
 
 def shards(fixed_image, moving_patches, owners, offsets, mobility, prior_flow):
-    meta = jnp.pad(jnp.concatenate([owners, offsets[0].T], axis=0), ((0, 5), (0, 96)))
     f32, bf16 = jnp.float32, jnp.bfloat16
     sds = jax.ShapeDtypeStruct
     dma = pltpu.SemaphoreType.DMA
@@ -587,9 +595,12 @@
             sds((2, ROWS, COLS), f32),
             sds((NP, SPAN, 128), f32),
         ),
-        in_specs=[hbm_spec(), hbm_spec(), vmem_spec(), hbm_spec(), hbm_spec()],
+        in_specs=[hbm_spec()] * 6,
         out_specs=(any_spec(), any_spec(), any_spec(), any_spec(), vmem_spec(), vmem_spec()),
         scratch_shapes=[
+            pltpu.VMEM((8, 128), jnp.int32),
+            pltpu.VMEM((1, PATCH_DEV), jnp.int32),
+            pltpu.VMEM((2, PATCH_DEV), jnp.int32),
             pltpu.VMEM((2, ROWS, COLS), f32),
             pltpu.VMEM((ROWS, COLS), f32),
             pltpu.VMEM((PATCH_DEV, W, W), bf16),
@@ -604,42 +615,38 @@
             pltpu.VMEM((NP, 1, 3, HIGH, 128), f32),
             pltpu.VMEM((NP, 2, ROWS, 128), f32),
             pltpu.VMEM((NP, 2, ROWS, 128), f32),
-            dma((5,)), dma((2, 6)), dma((2, 6)), dma((2, 8)), dma((2, 8)), dma((16,)), dma((16,)),
+            dma((6,)), dma((2, 6)), dma((2, 6)), dma((2, 8)), dma((2, 8)), dma((16,)), dma((16,)),
             dma((3,)), dma((3,)), dma((19,)), dma((19,)), dma((3,)), dma((3,)),
         ],
         compiler_params=pltpu.CompilerParams(
             collective_id=0, has_side_effects=True, vmem_limit_bytes=60 * 2**20
         ),
         name="gather_and_relax",
-    )(fixed_image[0], moving_patches[0], meta, prior_flow[0], mobility[0])
+    )(fixed_image[0], moving_patches[0], owners, offsets[0].T, prior_flow[0], mobility[0])
     ep = flow_call(gmeta, gi, gpl, gpr)
-    net = pl.pallas_call(
-        share_kernel,
-        out_shape=sds((NP, SPAN, 128), f32),
-        in_specs=[vmem_spec()],
-        out_specs=any_spec(),
-        scratch_shapes=[
-            pltpu.VMEM((3, ROWS, 128), f32), pltpu.VMEM((ROWS, 128), f32),
-            dma((3,)), dma((3,)), dma((19,)), dma((19,)), dma(()),
-        ],
-        compiler_params=pltpu.CompilerParams(collective_id=1, has_side_effects=True),
-        name="share_flows",
-    )(ep)
     flow, out = pl.pallas_call(
         settle_kernel,
         out_shape=(sds((2, PATCH_DEV), f32), sds((2, ROWS, COLS), f32)),
-        in_specs=[vmem_spec()] * 3,
+        in_specs=[vmem_spec(), any_spec(), any_spec()],
         out_specs=(vmem_spec(), vmem_spec()),
         scratch_shapes=[
+            pltpu.VMEM((3, ROWS, 128), f32),
+            pltpu.VMEM((ROWS, 128), f32),
+            pltpu.VMEM((NP, SPAN, 128), f32),
+            pltpu.VMEM((NP, SPAN, 128), f32),
+            pltpu.VMEM((2, ROWS, COLS), f32),
             pltpu.VMEM((NP, 2, 1, HIGH, 128), f32),
             pltpu.VMEM((NP, 1, HIGH, 128), f32),
             pltpu.VMEM((NP, 2, 1, HIGH, 128), f32),
             pltpu.VMEM((NP, 2, 1, HIGH, 128), f32),
             pltpu.VMEM((NP, 2, 1, HIGH, 128), f32),
+            dma((3,)), dma((3,)), dma((19,)), dma((19,)), dma((2,)),
         ],
-        compiler_params=pltpu.CompilerParams(vmem_limit_bytes=60 * 2**20),
-        name="settle",
-    )(net, mob_band, u_own)
+        compiler_params=pltpu.CompilerParams(
+            collective_id=1, has_side_effects=True, vmem_limit_bytes=32 * 2**20
+        ),
+        name="share_and_settle",
+    )(ep, mob_band, u_own)
     return flow[None], out[None]
 
 

time: 111 us -> 109 us (0.982); the launches traced: 111 us -> 107 us
  Pallas kernels: 109 us -> 105 us
  local copies, waits for them, and re-layouts: 0.6 us -> 1.96 us
    pallas_call x1 -> x0, Pallas kernels: 13.8 us -> none  [shards(): pl.pallas_call(share_kernel, out_shape=sds((NP, SPAN, 128), f32), in_spec...]
    pallas_call x1, Pallas kernels: 7.45 us -> 17.5 us  [shards(): pl.pallas_call(settle_kernel, out_shape=(sds((2, PATCH_DEV), f32), sds((2...]
    unnamed x0 -> x8, local copies, waits for them, and re-layouts: none -> 1.96 us
where the time goes in v4:
time: 109 us; the launch traced here: 107 us
  Pallas kernels  105 us (96%)
  local copies, waits for them, and re-layouts  1.96 us (2%)
    pallas_call x1, Pallas kernels, shards(): pl.pallas_call(gather_kernel, out_shape=(sds((NZ * NC, TILE, TILE), bf16)...  71.3 us
    pallas_call x1, Pallas kernels, shards(): pl.pallas_call(settle_kernel, out_shape=(sds((2, PATCH_DEV), f32), sds((2...  17.5 us
    pallas_call x1, Pallas kernels, flow_call(): pl.pallas_call(flow_kernel, out_shape=jax.ShapeDtypeStruct((NY, ROWS, 128...  15.9 us

profile of v4, /device:TPU:1, one launch (start us, length us, event | category | flops | bytes accessed | tf_op | source)
XLA Modules:
  0.0 107.3 jit_solution(10104430973532348520)
XLA Ops:
  0.6 71.3 %gather_and_relax.1 = (bf16[16,512,512]{2,1,0:T(8,128)(2,1)}, bf16[4,32,160,128]{3,2,1,0:T(8,128)(2,1)}, bf16[4,8,160,128]{3,2,1,0:T(8,128)(2,1)}, s32[4,8,128]{...) custom-call(bf16[512,512]{1,0:T(8,128)(2,1)} %bitcast.12, bf16[32,160,160]{2,1,0:T(8,128)(2,1)} %bitcast.11, ...), custom_call_target="tpu_custom_call" | custom-call | tf_op jit(solution)/shard_map/gather_and_relax/pallas_call | solution.py:588
  71.9 0.0 copy-start
  71.9 0.0 copy-start.2
  71.9 15.9 %patch_flows.1.ep = f32[4,16,128]{2,1,0:T(8,128)} custom-call(s32[4,8,128]{2,1,0:T(8,128)} %get-tuple-element.10.meta, bf16[16,512,512]{2,1,0:T(8,128)(2,1)} %get-tuple-element.11.gi, bf16[4,32,160,128]{3,2,1,0:T(8,128)(2,1)} %get-tuple-element.12.gpl, bf16[4,8,160,128]{3,2,1,0:T(8,128)(2,1)} %get-tuple-element.13.gpr, ...), custom_call_target="tpu_custom_call" | custom-call | tf_op jit(solution)/shard_map/patch_flows/pallas_call | solution.py:558
  87.8 0.0 copy-done
  87.8 0.0 copy-done.2
  87.9 0.0 copy-start.1
  87.9 0.7 copy-done.1
  88.6 17.5 %share_and_settle.1 = (f32[2,32]{1,0:T(2,128)S(1)}, f32[2,16,512]{2,1,0:T(8,128)S(1)}) custom-call(f32[4,16,128]{2,1,0:T(8,128)S(1)} %copy-done.1, f32[4,80,128]{2,1,0:T(8,128)S(1)} %copy-done, f32[2,16,512]{2,1,0:T(8,128)S(1)} %copy-done.2), custom_call_target="tpu_custom_call" | custom-call | tf_op jit(solution)/shard_map/share_and_settle/pallas_call | solution.py:627
  106.1 0.6 copy.14
  106.6 0.6 copy.15
Async XLA Ops:
  71.9 15.9 %copy-start = (f32[4,80,128]{2,1,0:T(8,128)S(1)}, f32[4,80,128]{2,1,0:T(8,128)}, u32[]{:S(2)}) copy-start(f32[4,80,128]{2,1,0:T(8,128)} %get-tuple-element.14.mob_hbm) | copy-start | bytes 491524
  71.9 15.9 %copy-start.2 = (f32[2,16,512]{2,1,0:T(8,128)S(1)}, f32[2,16,512]{2,1,0:T(8,128)}, u32[]{:S(2)}) copy-start(f32[2,16,512]{2,1,0:T(8,128)} %get-tuple-element.15.own_hbm) | copy-start | bytes 196612
  87.9 0.8 copy-start.1

commit v5 on v4

--- a/solution.py
+++ b/solution.py
@@ -157,11 +157,35 @@
     for v in range(NP):
         own[v, 0:3] = fine[v % 2, v // 2 : v // 2 + 3].astype(jnp.bfloat16)
         own[v, 3:7] = fine[2].astype(jnp.bfloat16)
-    meshes = []
-    for n, (dp, d, device) in enumerate(halo):
-        rows = pl.ds(ROWS * (2 - d), ROWS)
-        copy = remote(own.at[(p + dp) % NP], net.at[p, :, rows, :], hsend.at[n], hrecv.at[n], device)
+    e = 1 - 2 * c
+    meshes, shared = [], []
+
+    def strip_rows(d):
+        return pl.ds(pl.multiple_of(ROWS * (2 + d), ROWS), ROWS)
+
+    def send_strip(dp, d):
+        n = len(meshes)
+        device = {"tile": (t + d + TILES) % TILES, "pair": (p + dp) % NP}
+        copy = remote(own.at[(p + dp) % NP], net.at[p, :, strip_rows(-d), :], hsend.at[n], hrecv.at[n], device)
         start(copy, meshes)
+
+    for dp in range(NP):
+        send_strip(dp, -2 * e)
+    for dp in range(NP):
+        send_strip(dp, 2 * e)
+        send_strip(dp, e)
+        if dp:
+            send_strip(dp, 0)
+
+    def share_strips():
+        for dp in range(NP):
+            meshes[dp].wait_recv()
+            s = (p + NP - dp) % NP
+            n = len(meshes) + len(shared)
+            copy = remote(
+                net.at[s, :, strip_rows(2 * e), :], net.at[s, :, strip_rows(e), :], hsend.at[n], hrecv.at[n], sibling
+            )
+            start(copy, shared)
 
     start(y_left(lo, y, 0, right_y, 1), yr)
     start(y_left(hi, y, 1, left_y, 1), yl)
@@ -203,7 +227,7 @@
     comp, side = p % 2, p // 2
 
     def begin():
-        for copy in meshes:
+        for copy in meshes[NP:] + shared:
             copy.wait_recv()
         net[p, :, HALO : HALO + ROWS, :] = own[p]
         edge = jnp.zeros((NP, 1, 3, PAD, 128), jnp.float32)
@@ -249,6 +273,7 @@
     far = []
     forward_z(1, 0)
     forward_z(1, 1)
+    share_strips()
     forward_z(2, 0)
     forward_y()
     begin()

time: 109 us -> 109 us (level); the launches traced: 107 us -> 108 us
    pallas_call x1, Pallas kernels: 17.5 us -> 22.2 us  [shards(): pl.pallas_call(settle_kernel, out_shape=(sds((2, PATCH_DEV), f32), sds((2...]
    pallas_call x1, Pallas kernels: 15.9 us -> 13.5 us  [flow_call(): pl.pallas_call(flow_kernel, out_shape=jax.ShapeDtypeStruct((NY, ROWS, 128...]
    pallas_call x1, Pallas kernels: 71.3 us -> 70 us  [shards(): pl.pallas_call(gather_kernel, out_shape=(sds((NZ * NC, TILE, TILE), bf16)...]
where the time goes in v5:
time: 109 us; the launch traced here: 108 us
  Pallas kernels  106 us (97%)
  local copies, waits for them, and re-layouts  1.96 us (2%)
    pallas_call x1, Pallas kernels, shards(): pl.pallas_call(gather_kernel, out_shape=(sds((NZ * NC, TILE, TILE), bf16)...  70 us
    pallas_call x1, Pallas kernels, shards(): pl.pallas_call(settle_kernel, out_shape=(sds((2, PATCH_DEV), f32), sds((2...  22.2 us
    pallas_call x1, Pallas kernels, flow_call(): pl.pallas_call(flow_kernel, out_shape=jax.ShapeDtypeStruct((NY, ROWS, 128...  13.5 us

profile of v5, /device:TPU:1, one launch (start us, length us, event | category | flops | bytes accessed | tf_op | source)
XLA Modules:
  0.0 108.4 jit_solution(14681403900799419149)
XLA Ops:
  0.6 70.0 %gather_and_relax.1 = (bf16[16,512,512]{2,1,0:T(8,128)(2,1)}, bf16[4,32,160,128]{3,2,1,0:T(8,128)(2,1)}, bf16[4,8,160,128]{3,2,1,0:T(8,128)(2,1)}, s32[4,8,128]{...) custom-call(bf16[512,512]{1,0:T(8,128)(2,1)} %bitcast.12, bf16[32,160,160]{2,1,0:T(8,128)(2,1)} %bitcast.11, ...), custom_call_target="tpu_custom_call" | custom-call | tf_op jit(solution)/shard_map/gather_and_relax/pallas_call | solution.py:613
  70.7 0.0 copy-start
  70.7 0.0 copy-start.2
  70.7 13.5 %patch_flows.1.ep = f32[4,16,128]{2,1,0:T(8,128)} custom-call(s32[4,8,128]{2,1,0:T(8,128)} %get-tuple-element.10.meta, bf16[16,512,512]{2,1,0:T(8,128)(2,1)} %get-tuple-element.11.gi, bf16[4,32,160,128]{3,2,1,0:T(8,128)(2,1)} %get-tuple-element.12.gpl, bf16[4,8,160,128]{3,2,1,0:T(8,128)(2,1)} %get-tuple-element.13.gpr, ...), custom_call_target="tpu_custom_call" | custom-call | tf_op jit(solution)/shard_map/patch_flows/pallas_call | solution.py:583
  84.2 0.0 copy-done
  84.2 0.0 copy-done.2
  84.2 0.0 copy-start.1
  84.3 0.7 copy-done.1
  85.0 22.2 %share_and_settle.1 = (f32[2,32]{1,0:T(2,128)S(1)}, f32[2,16,512]{2,1,0:T(8,128)S(1)}) custom-call(f32[4,16,128]{2,1,0:T(8,128)S(1)} %copy-done.1, f32[4,80,128]{2,1,0:T(8,128)S(1)} %copy-done, f32[2,16,512]{2,1,0:T(8,128)S(1)} %copy-done.2), custom_call_target="tpu_custom_call" | custom-call | tf_op jit(solution)/shard_map/share_and_settle/pallas_call | solution.py:652
  107.2 0.6 copy.14
  107.8 0.6 copy.15
Async XLA Ops:
  70.7 13.6 %copy-start = (f32[4,80,128]{2,1,0:T(8,128)S(1)}, f32[4,80,128]{2,1,0:T(8,128)}, u32[]{:S(2)}) copy-start(f32[4,80,128]{2,1,0:T(8,128)} %get-tuple-element.14.mob_hbm) | copy-start | bytes 491524
  70.7 13.6 %copy-start.2 = (f32[2,16,512]{2,1,0:T(8,128)S(1)}, f32[2,16,512]{2,1,0:T(8,128)}, u32[]{:S(2)}) copy-start(f32[2,16,512]{2,1,0:T(8,128)} %get-tuple-element.15.own_hbm) | copy-start | bytes 196612
  84.2 0.8 copy-start.1
